TPU v7x, 32 devices: a whole 2x2x4 slice. The times are simulated.
32 devices in a mesh: fsdp: 4 (over z), ctx: 4 (over x, core), tp: 2 (over y).
Axes of the slice: x: 2, y: 2, z: 4, core: 2. Of those that a mesh axis runs over, the one named last changes fastest.
Arguments:
- tokens: bfloat16 [12, 1152, 1024], P('fsdp', 'ctx'), may hold values from -6 to 6
- segment_ids: int32 [12, 1152], P('fsdp'), may hold values from 0 to 3, as said below
- first_gain: float32 [1024], replicated, may hold values from 0.5 to 1.5
- first_shift: float32 [1024], replicated, may hold values from -1 to 1
- qkv_weight: bfloat16 [3, 1024, 1024], P(None, ('fsdp', 'ctx'), 'tp'), may hold values from -0.1875 to 0.1875
- qv_bias: float32 [2, 1024], P(None, 'tp'), may hold values from -1 to 1
- out_weight: bfloat16 [1024, 1024], P('tp', ('fsdp', 'ctx')), may hold values from -1.5 to 1.5
- out_bias: float32 [1024], replicated, may hold values from -1 to 1
- second_gain: float32 [1024], replicated, may hold values from 0.5 to 1.5
- second_shift: float32 [1024], replicated, may hold values from -1 to 1
- up_weight: bfloat16 [1024, 4096], P(('fsdp', 'ctx'), 'tp'), may hold values from -0.1875 to 0.1875
- up_bias: float32 [4096], P('tp'), may hold values from -1 to 1
- down_weight: bfloat16 [4096, 1024], P('tp', ('fsdp', 'ctx')), may hold values from -0.09375 to 0.09375
- down_bias: float32 [1024], replicated, may hold values from -1 to 1
- cotangent: bfloat16 [12, 1152, 1024], P('fsdp', 'ctx'), may hold values from -6 to 6
Outputs:
- layer_out: bfloat16 [12, 1152, 1024], P('fsdp', 'ctx')
- grad_tokens: float32 [12, 1152, 1024], P('fsdp', 'ctx')
- grad_first_gain: float32 [1024], replicated
- grad_first_shift: float32 [1024], replicated
- grad_qkv_weight: float32 [3, 1024, 1024], P(None, ('fsdp', 'ctx'), 'tp')
- grad_qv_bias: float32 [2, 1024], P(None, 'tp')
- grad_out_weight: float32 [1024, 1024], P('tp', ('fsdp', 'ctx'))
- grad_out_bias: float32 [1024], replicated
- grad_second_gain: float32 [1024], replicated
- grad_second_shift: float32 [1024], replicated
- grad_up_weight: float32 [1024, 4096], P(('fsdp', 'ctx'), 'tp')
- grad_up_bias: float32 [4096], P('tp')
- grad_down_weight: float32 [4096, 1024], P('tp', ('fsdp', 'ctx'))
- grad_down_bias: float32 [1024], replicated
Inputs may be any that keep to these rules, and one draw needn't show every extreme that they name: `segment_ids`: along each sequence the segment numbers never fall and start at 0. In each aligned block of 3 sequences one sequence is a single segment; in every other sequence the numbers rise by 3 in all.
All inputs are finite; a program needn't handle non-finite values.
Results may differ from a plain program's by a relative error of at most 0.013.
Values may be sent and summed in bfloat16 or wider, within the bound.
A program may use at most 192 MiB of HBM per device.

v0:
```python
import jax
import jax.numpy as jnp
from jax import lax
from jax.sharding import PartitionSpec as P

HD = 64
QBLK = 576


EPS = 1e-05
MASKED = -1e30


def smooth_gate(values):
    return jax.nn.gelu(values, approximate=True)


def norm_forward(values, gain, shift):
    centred = values - jnp.mean(values, -1, keepdims=True)
    spread = jnp.mean(centred * centred, -1, keepdims=True)
    inverse = lax.rsqrt(spread + EPS)
    normed = centred * inverse
    return (normed * gain + shift, normed, inverse)


def norm_backward(grad, normed, inverse, gain):
    grad_gain = jnp.sum(grad * normed, axis=(0, 1))
    grad_shift = jnp.sum(grad, axis=(0, 1))
    scaled = grad * gain
    first_mean = jnp.mean(scaled, -1, keepdims=True)
    second_mean = jnp.mean(scaled * normed, -1, keepdims=True)
    return (inverse * (scaled - first_mean - normed * second_mean), grad_gain, grad_shift)


def masked_scores(block_queries, key_heads, block_segments, segments, block_start, score_scale):
    scores = (
        jnp.einsum("qhd,khd->hqk", block_queries, key_heads, preferred_element_type=jnp.float32)
        * score_scale
    )
    row_pos = block_start + lax.iota(jnp.int32, block_queries.shape[0])
    col_pos = lax.iota(jnp.int32, key_heads.shape[0])
    allowed = (row_pos[:, None] >= col_pos[None, :]) & (
        block_segments[:, None] == segments[None, :]
    )
    return jnp.where(allowed[None], scores, MASKED)


def attend_forward(queries, key_heads, value_heads, segments, score_scale):
    seq_len = queries.shape[0]

    def one_block(block_index):
        block_start = block_index * QBLK
        block_queries = lax.dynamic_slice_in_dim(queries, block_start, QBLK, 0)
        block_segments = lax.dynamic_slice_in_dim(segments, block_start, QBLK, 0)
        scores = masked_scores(
            block_queries, key_heads, block_segments, segments, block_start, score_scale
        )
        highest = jnp.max(scores, -1, keepdims=True)
        raised = jnp.exp(scores - highest)
        summed = jnp.sum(raised, -1, keepdims=True)
        softmaxed = (raised / summed).astype(jnp.bfloat16)
        block_out = jnp.einsum(
            "hqk,khd->qhd", softmaxed, value_heads, preferred_element_type=jnp.float32
        )
        return (block_out, (highest + jnp.log(summed))[..., 0])

    block_outs, log_sums = lax.map(one_block, jnp.arange(seq_len // QBLK, dtype=jnp.int32))
    return (block_outs.reshape(seq_len, queries.shape[1], queries.shape[2]), log_sums)


def attend_backward(queries, key_heads, value_heads, segments, log_sums, grad_heads, score_scale):
    seq_len = queries.shape[0]
    empty_grad = jnp.zeros(key_heads.shape, jnp.float32)

    def one_block(carried, block_index):
        grad_keys, grad_values = carried
        block_start = block_index * QBLK
        block_queries = lax.dynamic_slice_in_dim(queries, block_start, QBLK, 0)
        block_segments = lax.dynamic_slice_in_dim(segments, block_start, QBLK, 0)
        block_grads = lax.dynamic_slice_in_dim(grad_heads, block_start, QBLK, 0)
        scores = masked_scores(
            block_queries, key_heads, block_segments, segments, block_start, score_scale
        )
        softmaxed = jnp.exp(scores - log_sums[block_index][..., None])
        grad_soft = jnp.einsum(
            "qhd,khd->hqk", block_grads, value_heads, preferred_element_type=jnp.float32
        )
        row_dot = jnp.sum(softmaxed * grad_soft, -1, keepdims=True)
        grad_scores = (softmaxed * (grad_soft - row_dot)).astype(jnp.bfloat16)
        grad_queries = (
            jnp.einsum("hqk,khd->qhd", grad_scores, key_heads, preferred_element_type=jnp.float32)
            * score_scale
        )
        grad_keys = (
            grad_keys
            + jnp.einsum(
                "hqk,qhd->khd", grad_scores, block_queries, preferred_element_type=jnp.float32
            )
            * score_scale
        )
        grad_values = grad_values + jnp.einsum(
            "hqk,qhd->khd",
            softmaxed.astype(jnp.bfloat16),
            block_grads,
            preferred_element_type=jnp.float32,
        )
        return ((grad_keys, grad_values), grad_queries)

    (grad_keys, grad_values), grad_queries = lax.scan(
        one_block, (empty_grad, empty_grad), jnp.arange(seq_len // QBLK, dtype=jnp.int32)
    )
    return (
        grad_queries.reshape(seq_len, queries.shape[1], queries.shape[2]),
        grad_keys,
        grad_values,
    )


def local(
    tokens,
    segment_ids,
    first_gain,
    first_shift,
    qkv_weight,
    qv_bias,
    out_weight,
    out_bias,
    second_gain,
    second_shift,
    up_weight,
    up_bias,
    down_weight,
    down_bias,
    cotangent,
):
    seq_count, local_len, model_width = tokens.shape
    seq_len = segment_ids.shape[1]
    score_scale = HD ** (-0.5)
    whole_qkv, whole_out, whole_up, whole_down = (
        lax.all_gather(qkv_weight, ("fsdp", "ctx"), axis=1, tiled=True),
        lax.all_gather(out_weight, ("fsdp", "ctx"), axis=1, tiled=True),
        lax.all_gather(up_weight, ("fsdp", "ctx"), axis=0, tiled=True),
        lax.all_gather(down_weight, ("fsdp", "ctx"), axis=1, tiled=True),
    )
    inputs = tokens.astype(jnp.float32)
    normed_in, normed_one, inverse_one = norm_forward(inputs, first_gain, first_shift)
    first_in = normed_in.astype(jnp.bfloat16)
    projected = jnp.einsum("scd,jde->scje", first_in, whole_qkv, preferred_element_type=jnp.float32)
    bias_rows = jnp.stack([qv_bias[0], jnp.zeros_like(qv_bias[0]), qv_bias[1]])
    projected = (projected + bias_rows).astype(jnp.bfloat16)
    by_heads = lax.all_to_all(projected, "ctx", split_axis=3, concat_axis=1, tiled=True)
    heads_width = by_heads.shape[3]
    heads_dev = heads_width // HD
    split_heads = by_heads.reshape(seq_count, seq_len, 3, heads_dev, HD)
    queries = split_heads[:, :, 0]
    key_heads = split_heads[:, :, 1]
    value_heads = split_heads[:, :, 2]

    def forward_member(member):
        return attend_forward(member[0], member[1], member[2], member[3], score_scale)

    attended, log_sums = lax.map(forward_member, (queries, key_heads, value_heads, segment_ids))
    attended = attended.reshape(seq_count, seq_len, heads_width).astype(jnp.bfloat16)
    mixed_heads = lax.all_to_all(attended, "ctx", split_axis=1, concat_axis=2, tiled=True)
    attn_part = jnp.einsum(
        "scf,fd->scd", mixed_heads, whole_out, preferred_element_type=jnp.float32
    )
    attn_full = lax.psum(attn_part, "tp")
    middle = inputs + attn_full + out_bias
    normed_mid, normed_two, inverse_two = norm_forward(middle, second_gain, second_shift)
    second_in = normed_mid.astype(jnp.bfloat16)
    hidden_pre = (
        jnp.einsum("scd,df->scf", second_in, whole_up, preferred_element_type=jnp.float32) + up_bias
    )
    activated, gate_pull = jax.vjp(smooth_gate, hidden_pre)
    hidden = activated.astype(jnp.bfloat16)
    down_part = jnp.einsum("scf,fd->scd", hidden, whole_down, preferred_element_type=jnp.float32)
    down_full = lax.psum(down_part.astype(jnp.bfloat16), "tp").astype(jnp.float32)
    layer_out = (middle + down_full + down_bias).astype(jnp.bfloat16)
    grad_top = cotangent.astype(jnp.float32)
    grad_down = jnp.einsum("scf,scd->fd", hidden, cotangent, preferred_element_type=jnp.float32)
    grad_down_b = jnp.sum(grad_top, axis=(0, 1))
    grad_hidden = jnp.einsum(
        "scd,fd->scf", cotangent, whole_down, preferred_element_type=jnp.float32
    )
    grad_pre = gate_pull(grad_hidden)[0]
    grad_up_b = jnp.sum(grad_pre, axis=(0, 1))
    grad_pre_low = grad_pre.astype(jnp.bfloat16)
    grad_up = jnp.einsum("scd,scf->df", second_in, grad_pre_low, preferred_element_type=jnp.float32)
    grad_norm_two = lax.psum(
        jnp.einsum("scf,df->scd", grad_pre_low, whole_up, preferred_element_type=jnp.float32), "tp"
    )
    grad_mid_norm, grad_gain_two, grad_shift_two = norm_backward(
        grad_norm_two, normed_two, inverse_two, second_gain
    )
    grad_mid = grad_top + grad_mid_norm
    grad_out_b = jnp.sum(grad_mid, axis=(0, 1))
    grad_mid_low = grad_mid.astype(jnp.bfloat16)
    grad_out = jnp.einsum(
        "scf,scd->fd", mixed_heads, grad_mid_low, preferred_element_type=jnp.float32
    )
    grad_mixed = jnp.einsum(
        "scd,fd->scf", grad_mid_low, whole_out, preferred_element_type=jnp.float32
    ).astype(jnp.bfloat16)
    grad_attended = lax.all_to_all(grad_mixed, "ctx", split_axis=2, concat_axis=1, tiled=True)
    grad_attended = grad_attended.reshape(seq_count, seq_len, heads_dev, HD)

    def backward_member(member):
        return attend_backward(
            member[0], member[1], member[2], member[3], member[4], member[5], score_scale
        )

    grad_queries, grad_keys, grad_values = lax.map(
        backward_member, (queries, key_heads, value_heads, segment_ids, log_sums, grad_attended)
    )
    grad_heads = (
        jnp.stack([grad_queries, grad_keys, grad_values], axis=2)
        .reshape(seq_count, seq_len, 3, heads_width)
        .astype(jnp.bfloat16)
    )
    grad_proj = lax.all_to_all(grad_heads, "ctx", split_axis=1, concat_axis=3, tiled=True)
    grad_qv_b = jnp.sum(grad_proj[:, :, 0::2].astype(jnp.float32), axis=(0, 1))
    grad_qkv = jnp.einsum("scd,scje->jde", first_in, grad_proj, preferred_element_type=jnp.float32)
    grad_norm_one = lax.psum(
        jnp.einsum(
            "scje,jde->scd", grad_proj, whole_qkv, preferred_element_type=jnp.float32
        ).astype(jnp.bfloat16),
        "tp",
    ).astype(jnp.float32)
    grad_in_norm, grad_gain_one, grad_shift_one = norm_backward(
        grad_norm_one, normed_one, inverse_one, first_gain
    )
    grad_inputs = grad_mid + grad_in_norm
    summed_small = lax.psum(
        (
            grad_gain_one,
            grad_shift_one,
            grad_qv_b,
            grad_out_b,
            grad_gain_two,
            grad_shift_two,
            grad_up_b,
            grad_down_b,
        ),
        ("fsdp", "ctx"),
    )
    owned_qkv, owned_out, owned_up, owned_down = (
        lax.psum_scatter(grad_qkv, ("fsdp", "ctx"), scatter_dimension=1, tiled=True),
        lax.psum_scatter(grad_out, ("fsdp", "ctx"), scatter_dimension=1, tiled=True),
        lax.psum_scatter(grad_up, ("fsdp", "ctx"), scatter_dimension=0, tiled=True),
        lax.psum_scatter(grad_down, ("fsdp", "ctx"), scatter_dimension=1, tiled=True),
    )
    (
        sum_gain_one,
        sum_shift_one,
        sum_qv_b,
        sum_out_b,
        sum_gain_two,
        sum_shift_two,
        sum_up_b,
        sum_down_b,
    ) = summed_small
    return (
        layer_out,
        grad_inputs,
        sum_gain_one,
        sum_shift_one,
        owned_qkv,
        sum_qv_b,
        owned_out,
        sum_out_b,
        sum_gain_two,
        sum_shift_two,
        owned_up,
        sum_up_b,
        owned_down,
        sum_down_b,
    )


def solution(mesh):
    return jax.shard_map(
        local,
        mesh=mesh,
        in_specs=(
            P("fsdp", "ctx", None),
            P("fsdp", None),
            P(),
            P(),
            P(None, ("fsdp", "ctx"), "tp"),
            P(None, "tp"),
            P("tp", ("fsdp", "ctx")),
            P(),
            P(),
            P(),
            P(("fsdp", "ctx"), "tp"),
            P("tp"),
            P("tp", ("fsdp", "ctx")),
            P(),
            P("fsdp", "ctx", None),
        ),
        out_specs=(
            P("fsdp", "ctx", None),
            P("fsdp", "ctx", None),
            P(),
            P(),
            P(None, ("fsdp", "ctx"), "tp"),
            P(None, "tp"),
            P("tp", ("fsdp", "ctx")),
            P(),
            P(),
            P(),
            P(("fsdp", "ctx"), "tp"),
            P("tp"),
            P("tp", ("fsdp", "ctx")),
            P(),
        ),
        check_vma=False,
    )
```

profile of v0, /device:TPU:0, one launch (start us, length us, event | category | flops | bytes accessed | tf_op | source)
XLA Modules:
  0.0 1361.2 jit_solution(8989010546299976332)
XLA Ops:
  12.8 45.4 %all-gather.5.cloned.1.call-done = bf16[3,1024,512]{2,1,0:T(8,128)(2,1)} async-done(((bf16[3,64,512]{2,1,0:T(8,128)(2,1)}), bf16[3,1024,512]{2,1,0:T(8,128)(2,1)}) %all-gather.5.cloned.1.call-update) | async-done | bytes 3145744 | tf_op jit(solution)/shard_map/all_gather | solution.py:140
  58.2 6.3 add_convert_fusion
  64.5 7.8 copy.54
  72.3 5.0 all-to-all-start
  78.1 56.6 %all-to-all-done = bf16[3,288,3,512]{1,2,0,3:T(4,128)(2,1)} async-done(((bf16[3,288,3,512]{1,2,0,3:T(4,128)(2,1)}), bf16[3,288,3,512]{1,2,0,3:T(4,128)(2,1)}, u32[]{:S(2)}, u32[]{:S(2)}) %all-to-all-start) | async-done | bytes 2654240 | tf_op jit(solution)/shard_map/all_to_all | solution.py:151
  134.6 5.7 copy.107
  147.2 49.6 %while.54 = (s32[]{:T(128)}, bf16[3,1152,2,64]{1,3,2,0:T(8,128)(2,1)S(1)}, f32[3,2,2,576]{3,2,1,0:T(2,128)}, bf16[3,1152,2,64]{1,3,2,0:T(8,128)(2,1)}, s32[3,115...) while((s32[]{:T(128)}, ...), condition=%wide.region_7.8_spmd, body=%wide.region_2.7_spmd.sunk | while | flops 352345536 | bytes 21925056 | solution.py:162
  150.0 11.9 while.57
  166.6 11.9 while.57
  183.1 11.9 while.57
  197.6 18.3 %all_to_all.66 = bf16[3,1152,128]{2,0,1:T(4,128)(2,1)S(1)} all-to-all(bf16[3,1152,128]{2,0,1:T(4,128)(2,1)S(1)} %copy.57), channel_id=1, replica_groups=mesh['fsdp'=4,'ctx'=4,'tp'=2] {'ctx'}, dimensions={1} | all-to-all | bytes 1769472 | tf_op jit(solution)/shard_map/all_to_all | solution.py:164
  216.1 4.4 fusion.76
  221.7 92.1 %all-reduce.8.cloned.1.call-done = f32[3,288,1024]{2,1,0:T(8,128)} async-done(((f32[3,288,1024]{2,1,0:T(8,128)}), f32[3,288,1024]{2,1,0:T(8,128)}) %all-reduce.8.cloned.1.call-update) | async-done | bytes 3538960 | tf_op jit(solution)/shard_map/psum | solution.py:168
  317.5 49.3 %all-gather.9.cloned.1.call-done = bf16[1024,2048]{1,0:T(8,128)(2,1)} async-done(((bf16[64,2048]{1,0:T(8,128)(2,1)}), bf16[1024,2048]{1,0:T(8,128)(2,1)}) %all-gather.9.cloned.1.call-update) | async-done | bytes 4194320 | tf_op jit(solution)/shard_map/all_gather | solution.py:142
  366.8 16.9 %fusion.48 = f32[3,288,2048]{2,1,0:T(8,128)} fusion(bf16[1024,2048]{1,0:T(8,128)(2,1)} %all-gather.9.cloned.1.call-done, f32[3,288,1024]{2,1,0:T(8,128)S(1)} %get-tuple-element.414, f32[1024]{0:T(1024)} %param.32, f32[1024]{0:T(1024)} %param.31, f32[3,288]{1,0:T(4,128)S(1)} %add_rsqrt_fusion, f32[3,288]{1,0:T(4,128)S(1)} %broadcast_multiply_fusion.4), kind=kOutput, calls=%fused_computation.87 | convolution fusion | flops 3628302336 | bytes 14826240 | tf_op jit(solution)/shard_map/scd,df->scf/dot_general | solution.py:173
  383.7 34.6 %all-gather.11.cloned.1.call-done = bf16[2048,1024]{0,1:T(8,128)(2,1)} async-done(((bf16[2048,64]{0,1:T(8,128)(2,1)}), bf16[2048,1024]{0,1:T(8,128)(2,1)}) %all-gather.11.cloned.1.call-update) | async-done | bytes 4194320 | tf_op jit(solution)/shard_map/all_gather | solution.py:143
  418.3 13.1 fusion.91
  433.1 5.7 fusion.46
  438.8 93.0 %all-reduce.10.cloned.1.call-done = f32[3,288,1024]{2,1,0:T(8,128)} async-done(((f32[3,288,1024]{2,1,0:T(8,128)}), f32[3,288,1024]{2,1,0:T(8,128)}) %all-reduce.10.cloned.1.call-update) | async-done | bytes 3538960 | tf_op jit(solution)/shard_map/psum | solution.py:190
  531.8 4.4 multiply_reduce_fusion.1
  543.9 3.6 all-to-all-start.2
  547.5 20.0 %all-to-all-done.2 = bf16[3,288,512]{1,0,2:T(4,128)(2,1)S(1)} async-done(((bf16[3,288,512]{1,0,2:T(4,128)(2,1)}), bf16[3,288,512]{1,0,2:T(4,128)(2,1)S(1)}, u32[]{:S(2)}, u32[]{:S(2)}) %all-to-all-start.2) | async-done | bytes 884768 | tf_op jit(solution)/shard_map/all_to_all | solution.py:205
  573.4 159.9 %while.56 = (s32[]{:T(128)}, bf16[3,1152,2,64]{1,3,2,0:T(8,128)(2,1)}, bf16[3,1152,2,64]{1,3,2,0:T(8,128)(2,1)}, bf16[3,1152,2,64]{1,3,2,0:T(8,128)(2,1)}, bf16[...) while((s32[]{:T(128)}, ...), condition=%wide.region_19.20_spmd, body=%wide.region_15.19_spmd.sunk | while | flops 864091584 | bytes 119795440 | solution.py:213
  578.9 43.1 %while.58 = (s32[]{:T(128)}, f32[1152,2,64]{0,2,1:T(8,128)S(1)}, f32[1152,2,64]{0,2,1:T(8,128)}, bf16[2,576,2,64]{1,3,2,0:T(8,128)(2,1)}, s32[2]{0:T(128)S(1)}, ...) while((s32[]{:T(128)}, f32[1152,2,64]{0,2,1:T(8,128)S(1)}, ...), condition=%wide.region_18.18_spmd.clone, body=%wide.region_16.17_spmd.clone.sunk | while | flops 864091584 | bytes 113278384 | solution.py:109
  586.3 5.0 multiply_reduce_fusion.6
  607.8 5.0 multiply_reduce_fusion.6
  632.1 43.1 %while.58 = (s32[]{:T(128)}, f32[1152,2,64]{0,2,1:T(8,128)S(1)}, f32[1152,2,64]{0,2,1:T(8,128)}, bf16[2,576,2,64]{1,3,2,0:T(8,128)(2,1)}, s32[2]{0:T(128)S(1)}, ...) while((s32[]{:T(128)}, f32[1152,2,64]{0,2,1:T(8,128)S(1)}, ...), condition=%wide.region_18.18_spmd.clone, body=%wide.region_16.17_spmd.clone.sunk | while | flops 864091584 | bytes 113278384 | solution.py:109
  639.6 5.0 multiply_reduce_fusion.6
  661.0 5.0 multiply_reduce_fusion.6
  685.4 43.1 %while.58 = (s32[]{:T(128)}, f32[1152,2,64]{0,2,1:T(8,128)S(1)}, f32[1152,2,64]{0,2,1:T(8,128)}, bf16[2,576,2,64]{1,3,2,0:T(8,128)(2,1)}, s32[2]{0:T(128)S(1)}, ...) while((s32[]{:T(128)}, f32[1152,2,64]{0,2,1:T(8,128)S(1)}, ...), condition=%wide.region_18.18_spmd.clone, body=%wide.region_16.17_spmd.clone.sunk | while | flops 864091584 | bytes 113278384 | solution.py:109
  692.9 5.0 multiply_reduce_fusion.6
  714.3 5.0 multiply_reduce_fusion.6
  733.3 3.6 pad_maximum_fusion
  736.8 6.0 copy.65
  742.8 44.1 %all_to_all.67 = bf16[3,1152,3,128]{3,0,2,1:T(4,128)(2,1)S(1)} all-to-all(bf16[3,1152,3,128]{3,0,2,1:T(4,128)(2,1)S(1)} %copy.65), channel_id=1, replica_groups=mesh['fsdp'=4,'ctx'=4,'tp'=2] {'ctx'}, dimensions={1} | all-to-all | bytes 5308416 | tf_op jit(solution)/shard_map/all_to_all | solution.py:221
  788.5 5.7 convolution_bitcast_fusion.2
  794.1 9.4 copy.68
  804.3 10.5 fusion.72
  814.8 4.1 bitcast_convert_fusion
  819.0 5.1 convolution_bitcast_fusion.3
  824.2 9.2 convolution_bitcast_fusion.1
  834.1 11.6 convolution_bitcast_fusion
  850.8 122.0 %all-reduce.12.cloned.1.call-done = f32[3,1024,512]{2,0,1:T(4,128)} async-done(((f32[3,1024,512]{2,0,1:T(4,128)}), f32[3,1024,512]{2,0,1:T(4,128)}) %all-reduce.12.cloned.1.call-update) | async-done | bytes 6291472
  974.8 95.4 %all-reduce.14.cloned.1.call-done = (bf16[3,288,1024]{2,1,0:T(8,128)(2,1)}, bf16[3,288,1024]{2,1,0:T(8,128)(2,1)}) async-done(((bf16[3,288,1024]{2,1,0:T(8,128)(2,1)}, bf16[3,288,1024]{2,1,0:T(8,128)(2,1)}), (bf16[3,288,1024]{2,1,0:T(8,128)(2,1)}, bf16[3,288,1024]{2,1,0:T(8,128)(2,1)})) %all-reduce.14.cloned.1.call-update) | async-done | bytes 3538960 | tf_op jit(solution)/shard_map/psum | solution.py:178
  1070.2 4.5 fusion.58
  1074.7 62.9 %all-reduce.1 = (f32[1024]{0:T(1024)}, f32[1024]{0:T(1024)}, f32[2,512]{1,0:T(2,128)}, f32[1024]{0:T(1024)}, f32[1024]{0:T(1024)}, /*index=5*/f32[1024]{0:T(1024)}, f32[2048]{0:T(1024)}, f32[1024]{0:T(1024)}) all-reduce(f32[1024]{0:T(1024)} %get-tuple-element.323, ...), channel_id=1, replica_groups=mesh['fsdp'=4,'ctx'=4,'tp'=2] {'fsdp','ctx'}, use_global_device_ids=true, to_apply=%region_24.25 | all-reduce | flops 9216 | bytes 73728 | tf_op jit(solution)/shard_map/psum | solution.py:234
  1145.7 99.2 %reduce-scatter.6.cloned.1.call-done = f32[64,2048]{1,0:T(8,128)} async-done(((f32[1024,2048]{1,0:T(8,128)}), f32[64,2048]{1,0:T(8,128)}) %reduce-scatter.6.cloned.1.call-update) | async-done | bytes 524304 | tf_op jit(solution)/shard_map/reduce_scatter | solution.py:250
  1244.9 109.6 %reduce-scatter.8.cloned.1.call-done = f32[2048,64]{0,1:T(8,128)} async-done(((f32[2048,1024]{0,1:T(8,128)}), f32[2048,64]{0,1:T(8,128)}) %reduce-scatter.8.cloned.1.call-update) | async-done | bytes 524304 | tf_op jit(solution)/shard_map/reduce_scatter | solution.py:251
  (482 shorter events, 209.8 us)
Async XLA Ops:
  7.2 51.0 %copy-start.10 = (bf16[3,288,1024]{2,1,0:T(8,128)(2,1)S(1)}, bf16[3,288,1024]{2,1,0:T(8,128)(2,1)}, u32[]{:S(2)}) copy-start(bf16[3,288,1024]{2,1,0:T(8,128)(2,1)} %param.23) | copy-start | bytes 5308420
  7.2 51.0 %copy-start.34 = (f32[1024]{0:T(1024)S(1)}, f32[1024]{0:T(1024)}, u32[]{:S(2)}) copy-start(f32[1024]{0:T(1024)} %param.25) | copy-start | bytes 12292
  7.2 51.0 %copy-start.42 = (f32[1024]{0:T(1024)S(1)}, f32[1024]{0:T(1024)}, u32[]{:S(2)}) copy-start(f32[1024]{0:T(1024)} %param.26) | copy-start | bytes 12292
  7.2 51.0 %all-gather.5.cloned.1.call-start = ((), (), s32[]{:S(2)}) async-start(), calls=%async_computation.7 | async-start | bytes 3342336 | tf_op jit(solution)/shard_map/all_gather | solution.py:140
  10.7 53.8 %copy-start.25 = (f32[3,288]{1,0:T(4,128)}, f32[3,288]{1,0:T(4,128)S(1)}, u32[]{:S(2)}) copy-start(f32[3,288]{1,0:T(4,128)S(1)} %broadcast_multiply_fusion.5) | copy-start | bytes 10372
  12.8 51.7 %copy-start.29 = (f32[3,288]{1,0:T(4,128)}, f32[3,288]{1,0:T(4,128)S(1)}, u32[]{:S(2)}) copy-start(f32[3,288]{1,0:T(4,128)S(1)} %add_rsqrt_fusion.1) | copy-start | bytes 10372
  72.3 62.3 %all-to-all-start = ((bf16[3,288,3,512]{1,2,0,3:T(4,128)(2,1)}), bf16[3,288,3,512]{1,2,0,3:T(4,128)(2,1)}, u32[]{:S(2)}, u32[]{:S(2)}) async-start(bf16[3,288,3,512]{1,2,0,3:T(4,128)(2,1)} %copy.54), calls=%async_computation | async-start | bytes 9437184 | tf_op jit(solution)/shard_map/all_to_all | solution.py:151
  77.3 138.8 %all-gather.7.cloned.1.call-start = ((), (), s32[]{:S(2)}) async-start(), calls=%async_computation.8 | async-start | bytes 1114112 | tf_op jit(solution)/shard_map/all_gather | solution.py:141
  78.0 235.8 %all-reduce.8.cloned.1.call-start = ((), (), s32[]{:S(2)}) async-start(), calls=%async_computation.9 | async-start | bytes 7077888 | tf_op jit(solution)/shard_map/psum | solution.py:168
  216.1 97.8 %copy-start.37 = (f32[1024]{0:T(1024)S(1)}, f32[1024]{0:T(1024)}, u32[]{:S(2)}) copy-start(f32[1024]{0:T(1024)} %param.30) | copy-start | bytes 12292
  220.5 146.3 %all-gather.9.cloned.1.call-start = ((), (), s32[]{:S(2)}) async-start(), calls=%async_computation.10 | async-start | bytes 4456448 | tf_op jit(solution)/shard_map/all_gather | solution.py:142
  221.1 197.2 %all-gather.11.cloned.1.call-start = ((), (), s32[]{:S(2)}) async-start(), calls=%async_computation.11 | async-start | bytes 4456448 | tf_op jit(solution)/shard_map/all_gather | solution.py:143
  221.7 310.1 %all-reduce.10.cloned.1.call-start = ((), (), s32[]{:S(2)}) async-start(), calls=%async_computation.12 | async-start | bytes 7077888 | tf_op jit(solution)/shard_map/psum | solution.py:190
  316.9 219.3 %copy-start.8 = (f32[3,288,1024]{2,1,0:T(8,128)}, f32[3,288,1024]{2,1,0:T(8,128)S(1)}, u32[]{:S(2)}) copy-start(f32[3,288,1024]{2,1,0:T(8,128)S(1)} %get-tuple-element.414) | copy-start | bytes 10616836
  316.9 219.3 %copy-start.27 = (f32[3,288]{1,0:T(4,128)}, f32[3,288]{1,0:T(4,128)S(1)}, u32[]{:S(2)}) copy-start(f32[3,288]{1,0:T(4,128)S(1)} %broadcast_multiply_fusion.4) | copy-start | bytes 10372
  317.5 218.7 %copy-start.32 = (f32[3,288]{1,0:T(4,128)}, f32[3,288]{1,0:T(4,128)S(1)}, u32[]{:S(2)}) copy-start(f32[3,288]{1,0:T(4,128)S(1)} %add_rsqrt_fusion) | copy-start | bytes 10372
  418.3 14.8 %copy-start.38 = (bf16[1024,2048]{1,0:T(8,128)(2,1)S(1)}, bf16[1024,2048]{1,0:T(8,128)(2,1)}, u32[]{:S(2)}) copy-start(bf16[1024,2048]{1,0:T(8,128)(2,1)} %all-gather.9.cloned.1.call-done) | copy-start | bytes 12582916
  543.9 23.6 %all-to-all-start.2 = ((bf16[3,288,512]{1,0,2:T(4,128)(2,1)}), bf16[3,288,512]{1,0,2:T(4,128)(2,1)S(1)}, u32[]{:S(2)}, u32[]{:S(2)}) async-start(bf16[3,288,512]{1,0,2:T(4,128)(2,1)} %copy.60), calls=%async_computation.2 | async-start | bytes 3145728 | tf_op jit(solution)/shard_map/all_to_all | solution.py:205
  547.5 425.3 %all-reduce.12.cloned.1.call-start = ((), (), s32[]{:S(2)}) async-start(), calls=%async_computation.16 | async-start | bytes 16777216
  578.9 12.5 copy-start.2
  578.9 12.5 copy-start.6
  578.9 12.5 copy-start.4
  600.3 12.5 copy-start.2
  600.3 12.5 copy-start.6
  600.4 12.5 copy-start.21
  600.4 12.5 copy-start.4
  632.1 12.5 copy-start.2
  632.2 12.5 copy-start.6
  632.2 12.5 copy-start.21
  632.2 12.5 copy-start.4
  653.6 12.5 copy-start.2
  653.6 12.5 copy-start.6
  653.6 12.5 copy-start.21
  653.7 12.5 copy-start.4
  685.4 12.5 copy-start.2
  685.5 12.5 copy-start.6
  685.5 12.5 copy-start.21
  685.5 12.5 copy-start.4
  706.9 12.5 copy-start.2
  706.9 12.5 copy-start.6
  706.9 12.5 copy-start.21
  706.9 12.5 copy-start.4
  787.3 27.5 %copy-start.16 = (bf16[3,1152,3,128]{3,1,2,0:T(8,128)(2,1)}, bf16[3,1152,3,128]{3,1,2,0:T(8,128)(2,1)S(1)}, u32[]{:S(2)}) copy-start(bf16[3,1152,3,128]{3,1,2,0:T(8,128)(2,1)S(1)} %copy.66) | copy-start | bytes 7962628
  803.6 266.6 %all-reduce.14.cloned.1.call-start = ((), (), s32[]{:S(2)}) async-start(), calls=%async_computation.17 | async-start | bytes 7077888 | tf_op jit(solution)/shard_map/psum | solution.py:178
  819.0 326.8 %reduce-scatter.4.cloned.1.call-start = ((), (), s32[]{:S(2)}) async-start(), calls=%async_computation.13 | async-start | bytes 2228224 | tf_op jit(solution)/shard_map/reduce_scatter | solution.py:249
  824.1 420.8 %reduce-scatter.6.cloned.1.call-start = ((), (), s32[]{:S(2)}) async-start(), calls=%async_computation.14 | async-start | bytes 8912896 | tf_op jit(solution)/shard_map/reduce_scatter | solution.py:250
  833.4 521.1 %reduce-scatter.8.cloned.1.call-start = ((), (), s32[]{:S(2)}) async-start(), calls=%async_computation.15 | async-start | bytes 8912896 | tf_op jit(solution)/shard_map/reduce_scatter | solution.py:251
  847.6 222.6 %copy-start.31 = (f32[3,288]{1,0:T(4,128)S(1)}, f32[3,288]{1,0:T(4,128)}, u32[]{:S(2)}) copy-start(f32[3,288]{1,0:T(4,128)} %copy-done.29) | copy-start | bytes 10372
  (83 other events, 288.3 us)
Sparse Core Ops, SparseCore 0:
  10.2 47.8 all-gather.4
  80.3 40.4 all-gather.6
  220.6 93.1 all-reduce.7
  316.1 50.7 all-gather.8
  369.1 49.2 all-gather.10
  438.9 92.8 all-reduce.9
  803.7 169.0 all-reduce.11
  975.8 94.3 all-reduce.13
  1074.5 61.6 reduce-scatter.3
  1141.3 103.6 reduce-scatter.5
  1250.1 104.3 reduce-scatter.7
where the time goes:
time: 1370 us; the launch traced here: 1360 us
  waiting for transfers between devices  820 us (60%)
  matrix products  193 us (14%)
  local copies, waits for them, and re-layouts  130 us (9%)
  blocking collectives  125 us (9%)
  other arithmetic  47.8 us (3%)
  loops' own time  21.4 us (2%)
  between operations  15.1 us (1%)
    unnamed x12, waiting for transfers between devices  125 us
    reduce_scatter x1, waiting for transfers between devices, local(): lax.psum_scatter(grad_down, ('fsdp', 'ctx'), scatter_dimension=1, tiled=T...  110 us
    reduce_scatter x1, waiting for transfers between devices, local(): lax.psum_scatter(grad_up, ('fsdp', 'ctx'), scatter_dimension=0, tiled=True)  99.2 us
    psum x1, waiting for transfers between devices, local(): lax.psum(down_part.astype(jnp.bfloat16), 'tp').astype(jnp.float32)  95.4 us
    psum x1, waiting for transfers between devices, local(): lax.psum(jnp.einsum('scf,df->scd', grad_pre_low, whole_up, preferred_elem...  93 us
    psum x1, waiting for transfers between devices, local(): attn_full = lax.psum(attn_part, 'tp')  92.1 us
    psum x1, blocking collectives, local(): lax.psum((grad_gain_one, grad_shift_one, grad_qv_b, grad_out_b, grad_gain...  62.9 us
    all_to_all x1, waiting for transfers between devices, local(): lax.all_to_all(projected, 'ctx', split_axis=3, concat_axis=1, tiled=True)  56.6 us
  transfers between devices with their start and end apart: 13, of which 11 were waited for; matrix products, arithmetic and copies ran while one was open for 10% of the time, Pallas kernels for 0%

commit v1 on v0

v1 whole, which is shorter than its diff:
```python
import functools

import jax
import jax.numpy as jnp
import numpy as np
from jax import lax
from jax.experimental import pallas as pl
from jax.experimental.pallas import tpu as pltpu
from jax.sharding import Mesh
from jax.sharding import PartitionSpec as P

HD = 64
EPS = 1e-05
MASKED = -1e30
LOG2E = 1.4426950408889634
BF = jnp.bfloat16
F32 = jnp.float32
CTX = ("x", "core")
SAME = ("fsdp", "x")
ALL = ("fsdp", "x", "core")


def smooth_gate(values):
    return jax.nn.gelu(values, approximate=True)


def norm_forward(values, gain, shift):
    centred = values - jnp.mean(values, -1, keepdims=True)
    spread = jnp.mean(centred * centred, -1, keepdims=True)
    inverse = lax.rsqrt(spread + EPS)
    normed = centred * inverse
    return (normed * gain + shift, normed, inverse)


def norm_backward(grad, normed, inverse, gain):
    grad_gain = jnp.sum(grad * normed, axis=(0, 1))
    grad_shift = jnp.sum(grad, axis=(0, 1))
    scaled = grad * gain
    first_mean = jnp.mean(scaled, -1, keepdims=True)
    second_mean = jnp.mean(scaled * normed, -1, keepdims=True)
    return (inverse * (scaled - first_mean - normed * second_mean), grad_gain, grad_shift)


def dot(a, b, da, db):
    return lax.dot_general(a, b, (((da,), (db,)), ((), ())), preferred_element_type=F32)


def query_block(seq_len):
    for size in (384, 256, 128, 64, 32, 16):
        if seq_len % size == 0:
            return size
    return seq_len


def masked_scores(k, q, start, first):
    keys, rows = k.shape[0], q.shape[0]
    scores = dot(k, q, 1, 1) * (HD ** (-0.5) * LOG2E)
    key_pos = lax.broadcasted_iota(jnp.int32, (keys, rows), 0)
    row_pos = first + lax.broadcasted_iota(jnp.int32, (1, rows), 1)
    allowed = (key_pos >= start) & (key_pos <= row_pos)
    return jnp.where(allowed, scores, MASKED)


def forward_kernel(q_ref, k_ref, v_ref, start_ref, out_ref, lse_ref):
    seq_len, width = q_ref.shape[1:]
    block = query_block(seq_len)
    for first in range(0, seq_len, block):
        rows = slice(first, first + block)
        keys = slice(0, first + block)
        start = start_ref[0, :, rows]
        for head in range(width // HD):
            cols = slice(head * HD, (head + 1) * HD)
            scores = masked_scores(k_ref[0, keys, cols], q_ref[0, rows, cols], start, first)
            highest = jnp.max(scores, 0, keepdims=True)
            raised = jnp.exp2(scores - highest)
            summed = jnp.sum(raised, 0, keepdims=True)
            probs = (raised * (1.0 / summed)).astype(BF)
            out_ref[0, rows, cols] = dot(probs, v_ref[0, keys, cols], 0, 0).astype(BF)
            lse_ref[0, head : head + 1, rows] = highest + jnp.log2(summed)


def backward_kernel(q_ref, k_ref, v_ref, start_ref, lse_ref, g_ref, dq_ref, dk_ref, dv_ref, ak, av):
    seq_len, width = q_ref.shape[1:]
    block = query_block(seq_len)
    ak[...] = jnp.zeros_like(ak)
    av[...] = jnp.zeros_like(av)
    for first in range(0, seq_len, block):
        rows = slice(first, first + block)
        keys = slice(0, first + block)
        start = start_ref[0, :, rows]
        for head in range(width // HD):
            cols = slice(head * HD, (head + 1) * HD)
            k, q, g = k_ref[0, keys, cols], q_ref[0, rows, cols], g_ref[0, rows, cols]
            scores = masked_scores(k, q, start, first)
            probs = jnp.exp2(scores - lse_ref[0, head : head + 1, rows])
            grad_probs = dot(v_ref[0, keys, cols], g, 1, 1)
            row_dot = jnp.sum(probs * grad_probs, 0, keepdims=True)
            grad_scores = (probs * (grad_probs - row_dot)).astype(BF)
            dq_ref[0, rows, cols] = (dot(grad_scores, k, 0, 0) * HD ** (-0.5)).astype(BF)
            ak[head, keys, :] += dot(grad_scores, q, 1, 0)
            av[head, keys, :] += dot(probs.astype(BF), g, 1, 0)
    for head in range(width // HD):
        cols = slice(head * HD, (head + 1) * HD)
        dk_ref[0, :, cols] = (ak[head] * HD ** (-0.5)).astype(BF)
        dv_ref[0, :, cols] = av[head].astype(BF)


def part_spec(seq_len, width, part):
    return pl.BlockSpec((1, seq_len, width), lambda s: (s, 0, part))


def attend_forward(q, k, v, start):
    seqs, seq_len, width = q.shape
    heads = width // HD
    whole = pl.BlockSpec((1, seq_len, width), lambda s: (s, 0, 0))
    row = pl.BlockSpec((1, 1, seq_len), lambda s: (s, 0, 0))
    lse = pl.BlockSpec((1, heads, seq_len), lambda s: (s, 0, 0))
    square = seqs * heads * seq_len * seq_len
    return pl.pallas_call(
        forward_kernel,
        grid=(seqs,),
        in_specs=[whole, whole, whole, row],
        out_specs=[whole, lse],
        out_shape=[
            jax.ShapeDtypeStruct((seqs, seq_len, width), BF),
            jax.ShapeDtypeStruct((seqs, heads, seq_len), F32),
        ],
        compiler_params=pltpu.CompilerParams(vmem_limit_bytes=40 * 1024 * 1024),
        cost_estimate=pl.CostEstimate(
            flops=square * HD * 16, bytes_accessed=seqs * seq_len * width * 8, transcendentals=square
        ),
    )(q, k, v, start)


def attend_backward(q, k, v, start, lses, grads):
    seqs, seq_len, width = q.shape
    heads = width // HD
    whole = pl.BlockSpec((1, seq_len, width), lambda s: (s, 0, 0))
    row = pl.BlockSpec((1, 1, seq_len), lambda s: (s, 0, 0))
    lse = pl.BlockSpec((1, heads, seq_len), lambda s: (s, 0, 0))
    square = seqs * heads * seq_len * seq_len
    shape = jax.ShapeDtypeStruct((seqs, seq_len, width), BF)
    return pl.pallas_call(
        backward_kernel,
        grid=(seqs,),
        in_specs=[whole, whole, whole, row, lse, whole],
        out_specs=[whole, whole, whole],
        out_shape=[shape, shape, shape],
        scratch_shapes=[
            pltpu.VMEM((heads, seq_len, HD), F32),
            pltpu.VMEM((heads, seq_len, HD), F32),
        ],
        compiler_params=pltpu.CompilerParams(vmem_limit_bytes=40 * 1024 * 1024),
        cost_estimate=pl.CostEstimate(
            flops=square * HD * 40, bytes_accessed=seqs * seq_len * width * 14, transcendentals=square
        ),
    )(q, k, v, start, lses, grads)


def swap(values, axis):
    count = lax.axis_size(axis)
    return lax.ppermute(values, axis, [(i, i ^ 1) for i in range(count)])


def pair_sum(values):
    sent = values.astype(BF)
    return sent.astype(F32) + swap(sent, "tp").astype(F32)


def gather_rows(shard):
    part = lax.all_gather(shard, SAME, axis=0, tiled=False)
    other = swap(part, "core")
    core = lax.axis_index("core")
    low = jnp.where(core == 0, part, other)
    high = jnp.where(core == 0, other, part)
    return jnp.stack([low, high], axis=1).reshape(-1, shard.shape[1])


def scatter_rows(grad):
    groups = lax.axis_size("fsdp") * lax.axis_size("x")
    rows = grad.shape[0] // (2 * groups)
    core = lax.axis_index("core")
    halves = grad.astype(BF).reshape(groups, 2, rows, grad.shape[1])
    mine = lax.dynamic_index_in_dim(halves, core, 1, keepdims=False)
    theirs = lax.dynamic_index_in_dim(halves, 1 - core, 1, keepdims=False)
    summed = (mine.astype(F32) + swap(theirs, "core").astype(F32)).astype(BF)
    summed = summed.reshape(groups * rows, grad.shape[1])
    return lax.psum_scatter(summed, SAME, scatter_dimension=0, tiled=True).astype(F32)


def small_sums(*vectors):
    flat = jnp.concatenate([v.reshape(-1) for v in vectors])
    total = jnp.sum(lax.all_gather(flat, ALL, axis=0, tiled=False), 0)
    outs, at = [], 0
    for v in vectors:
        outs.append(total[at : at + v.size].reshape(v.shape))
        at += v.size
    return outs


def local(
    tokens,
    segment_ids,
    first_gain,
    first_shift,
    qkv_weight,
    qv_bias,
    out_weight,
    out_bias,
    second_gain,
    second_shift,
    up_weight,
    up_bias,
    down_weight,
    down_bias,
    cotangent,
):
    seqs, local_len, model = tokens.shape
    seq_len = segment_ids.shape[1]
    heads_cols = qkv_weight.shape[2]
    rows = seqs * local_len
    barrier = lax.optimization_barrier
    qkv_rows = jnp.moveaxis(qkv_weight, 0, 1).reshape(qkv_weight.shape[1], 3 * heads_cols)
    w_qkv = gather_rows(qkv_rows)
    w_out = gather_rows(out_weight.T)
    w_up = gather_rows(up_weight)
    w_down = gather_rows(down_weight.T)

    start = jnp.sum(
        (segment_ids[:, None, :] < segment_ids[:, :, None]).astype(jnp.int32), -1
    )[:, None, :]
    inputs = tokens.astype(F32)
    normed_in, normed_one, inverse_one = norm_forward(inputs, first_gain, first_shift)
    first_in = normed_in.astype(BF)
    bias_row = jnp.concatenate([qv_bias[0], jnp.zeros_like(qv_bias[0]), qv_bias[1]])
    projected = (dot(first_in.reshape(rows, model), w_qkv, 1, 0) + bias_row).astype(BF)
    projected = projected.reshape(seqs, local_len, 3, heads_cols)
    by_heads = lax.all_to_all(projected, CTX, split_axis=3, concat_axis=1, tiled=True)
    q, k, v = by_heads[:, :, 0], by_heads[:, :, 1], by_heads[:, :, 2]
    attended, lses = attend_forward(q, k, v, start)
    mixed = lax.all_to_all(attended, CTX, split_axis=1, concat_axis=2, tiled=True)
    mixed_rows = mixed.reshape(rows, heads_cols)

    attn_part = dot(mixed_rows, w_out, 1, 1).reshape(seqs, local_len, model)
    cot_rows = cotangent.reshape(rows, model)
    middle = inputs + pair_sum(attn_part) + out_bias
    normed_mid, normed_two, inverse_two = norm_forward(middle, second_gain, second_shift)
    second_in = normed_mid.astype(BF).reshape(rows, model)
    hidden_pre = dot(second_in, w_up, 1, 0) + up_bias
    activated, gate_pull = jax.vjp(smooth_gate, hidden_pre)
    hidden = activated.astype(BF)
    grad_hidden = dot(cot_rows, w_down, 1, 0)
    grad_pre = gate_pull(grad_hidden)[0]
    grad_pre_low = grad_pre.astype(BF)
    grad_up_b = jnp.sum(grad_pre, axis=0)
    grad_two_sum = pair_sum(dot(grad_pre_low, w_up, 1, 1).reshape(seqs, local_len, model))
    grad_top = cotangent.astype(F32)
    grad_mid_norm, grad_gain_two, grad_shift_two = norm_backward(
        grad_two_sum, normed_two, inverse_two, second_gain
    )
    grad_mid = grad_top + grad_mid_norm
    grad_mid_low = grad_mid.astype(BF).reshape(rows, model)
    grad_mixed = dot(grad_mid_low, w_out, 1, 0).astype(BF).reshape(seqs, local_len, heads_cols)

    grad_down = dot(cot_rows, hidden, 0, 0).astype(BF)
    grad_up = dot(second_in, grad_pre_low, 0, 0).astype(BF)
    grad_out = dot(grad_mid_low, mixed_rows, 0, 0).astype(BF)
    down_part = dot(hidden, w_down, 1, 1).reshape(seqs, local_len, model)

    grad_att = lax.all_to_all(grad_mixed, CTX, split_axis=2, concat_axis=1, tiled=True)
    grad_att, grad_down, grad_up, grad_out, down_part = barrier(
        (grad_att, grad_down, grad_up, grad_out, down_part.astype(BF))
    )
    layer_out = (middle + pair_sum(down_part) + down_bias).astype(BF)
    dq, dk, dv = attend_backward(q, k, v, start, lses, grad_att)
    grad_heads = jnp.stack([dq, dk, dv], axis=2)
    grad_proj = lax.all_to_all(grad_heads, CTX, split_axis=1, concat_axis=3, tiled=True)
    grad_proj = grad_proj.reshape(rows, 3 * heads_cols)
    grad_one_part = dot(grad_proj, w_qkv, 1, 1).reshape(seqs, local_len, model)
    grad_one_sum = pair_sum(grad_one_part)
    grad_qkv = dot(first_in.reshape(rows, model), grad_proj, 0, 0)
    grad_in_norm, grad_gain_one, grad_shift_one = norm_backward(
        grad_one_sum, normed_one, inverse_one, first_gain
    )
    grad_inputs = grad_mid + grad_in_norm

    own_down = scatter_rows(grad_down).T
    own_up = scatter_rows(grad_up)
    own_out = scatter_rows(grad_out).T
    own_qkv = scatter_rows(grad_qkv)
    own_qkv = jnp.moveaxis(own_qkv.reshape(-1, 3, heads_cols), 1, 0)
    grad_qv_b = jnp.sum(grad_proj.astype(F32), axis=0).reshape(3, heads_cols)[0::2]
    sum_up_b, sum_down_b, sum_out_b, sum_gain_two, sum_shift_two = small_sums(
        grad_up_b,
        jnp.sum(grad_top, axis=(0, 1)),
        jnp.sum(grad_mid, axis=(0, 1)),
        grad_gain_two,
        grad_shift_two,
    )
    sum_qv_b, sum_gain_one, sum_shift_one = small_sums(grad_qv_b, grad_gain_one, grad_shift_one)
    return (
        layer_out,
        grad_inputs,
        sum_gain_one,
        sum_shift_one,
        own_qkv,
        sum_qv_b,
        own_out,
        sum_out_b,
        sum_gain_two,
        sum_shift_two,
        own_up,
        sum_up_b,
        own_down,
        sum_down_b,
    )


def solution(mesh):
    sizes = mesh.shape
    fine = Mesh(
        np.asarray(mesh.devices).reshape(sizes["fsdp"], sizes["ctx"] // 2, 2, sizes["tp"]),
        ("fsdp", "x", "core", "tp"),
    )
    return jax.shard_map(
        local,
        mesh=fine,
        in_specs=(
            P("fsdp", CTX, None),
            P("fsdp", None),
            P(),
            P(),
            P(None, ALL, "tp"),
            P(None, "tp"),
            P("tp", ALL),
            P(),
            P(),
            P(),
            P(ALL, "tp"),
            P("tp"),
            P("tp", ALL),
            P(),
            P("fsdp", CTX, None),
        ),
        out_specs=(
            P("fsdp", CTX, None),
            P("fsdp", CTX, None),
            P(),
            P(),
            P(None, ALL, "tp"),
            P(None, "tp"),
            P("tp", ALL),
            P(),
            P(),
            P(),
            P(ALL, "tp"),
            P("tp"),
            P("tp", ALL),
            P(),
        ),
        check_vma=False,
    )
```

time: 1370 us -> 683 us (0.50)
  waiting for transfers between devices: 820 us -> 247 us
  matrix products: 193 us -> 66.5 us
  local copies, waits for them, and re-layouts: 130 us -> 94.3 us
  Pallas kernels: 0 us -> 35.5 us
  loops' own time: 21.4 us -> 0 us
  starting transfers between devices: 9.15 us -> 24.4 us
  other arithmetic: 47.8 us -> 61.7 us
    psum x3 -> x0, waiting for transfers between devices: 281 us -> none  [the longest x1 95.4 us: local(): lax.psum(down_part.astype(jnp.bfloat16), 'tp').astype(jnp.float32)]
    reduce_scatter x3 -> x4, waiting for transfers between devices: 209 us -> 39 us  [scatter_rows(): lax.psum_scatter(summed, SAME, scatter_dimension=0, tiled=True).astype(F32)]
    all_gather x0 -> x3, blocking collectives: none -> 133 us  [the longest x1 94.5 us: gather_rows(): part = lax.all_gather(shard, SAME, axis=0, tiled=False)]
    dot_general x54 -> x12, matrix products: 193 us -> 66.5 us  [dot(): lax.dot_general(a, b, (((da,), (db,)), ((), ())), preferred_element_type=...]
    unnamed x12 -> x7, waiting for transfers between devices: 125 us -> 0.79 us
    ppermute x0 -> x12, waiting for transfers between devices: none -> 93.3 us  [swap(): return lax.ppermute(values, axis, [(i, i ^ 1) for i in range(count)])]
    all_gather x4 -> x3, waiting for transfers between devices: 129 us -> 47.5 us  [gather_rows(): part = lax.all_gather(shard, SAME, axis=0, tiled=False)]
    psum x1 -> x0, blocking collectives: 62.9 us -> none  [local(): lax.psum((grad_gain_one, grad_shift_one, grad_qv_b, grad_out_b, grad_gain...]
  transfers between devices with their start and end apart: 13 -> 23, of which waited for: 11 -> 10; matrix products, arithmetic and copies ran while one was open for 10% -> 25% of each run, Pallas kernels for 0% -> 5%
where the time goes in v1:
time: 683 us; the launch traced here: 677 us
  waiting for transfers between devices  247 us (36%)
  blocking collectives  133 us (19%)
  local copies, waits for them, and re-layouts  94.3 us (14%)
  matrix products  66.5 us (10%)
  other arithmetic  61.7 us (9%)
  Pallas kernels  35.5 us (5%)
  starting transfers between devices  24.4 us (4%)
  between operations  15 us (2%)
    all_gather x1, blocking collectives, gather_rows(): part = lax.all_gather(shard, SAME, axis=0, tiled=False)  94.5 us
    ppermute x12, waiting for transfers between devices, swap(): return lax.ppermute(values, axis, [(i, i ^ 1) for i in range(count)])  93.3 us
    dot_general x12, matrix products, dot(): lax.dot_general(a, b, (((da,), (db,)), ((), ())), preferred_element_type=...  66.5 us
    all_gather x3, waiting for transfers between devices, gather_rows(): part = lax.all_gather(shard, SAME, axis=0, tiled=False)  47.5 us
    all_to_all x1, waiting for transfers between devices, local(): lax.all_to_all(grad_heads, CTX, split_axis=1, concat_axis=3, tiled=True)  44.4 us
    reduce_scatter x4, waiting for transfers between devices, scatter_rows(): lax.psum_scatter(summed, SAME, scatter_dimension=0, tiled=True).astype(F32)  39 us
    all_gather x2, blocking collectives, small_sums(): total = jnp.sum(lax.all_gather(flat, ALL, axis=0, tiled=False), 0)  38.4 us
    pallas_call x1, Pallas kernels, attend_backward(): pl.pallas_call(backward_kernel, grid=(seqs,), in_specs=[whole, whole, who...  21.5 us
  transfers between devices with their start and end apart: 23, of which 10 were waited for; matrix products, arithmetic and copies ran while one was open for 25% of the time, Pallas kernels for 5%

profile of v1, /device:TPU:0, one launch (start us, length us, event | category | flops | bytes accessed | tf_op | source)
XLA Modules:
  0.0 677.5 jit_solution(3579735677780876976)
XLA Ops:
  10.2 47.5 %all-gather.9.cloned.1.call-done = bf16[8,64,1536]{2,1,0:T(8,128)(2,1)} async-done(((bf16[1,64,1536]{2,1,0:T(8,128)(2,1)}), bf16[8,64,1536]{2,1,0:T(8,128)(2,1)}) %all-gather.9.cloned.1.call-update) | async-done | bytes 1572880 | tf_op jit(solution)/shard_map/all_gather | solution.py:171
  64.4 4.2 add_convert_fusion
  68.6 5.8 reshape.182
  74.4 7.3 %copy.84 = bf16[3,288,3,512]{1,2,0,3:T(4,128)(2,1)} copy(bf16[3,288,3,512]{3,2,1,0:T(4,128)(2,1)S(1)} %reshape.182) | data formatting | bytes 5308416 | tf_op jit(solution)/shard_map/reshape | solution.py:237
  81.7 5.1 all-to-all-start
  86.8 94.5 %all-gather = bf16[512,512]{1,0:T(8,128)(2,1)S(1)} all-gather(bf16[64,512]{1,0:T(8,128)(2,1)S(1)} %bitcast.202), channel_id=2, replica_groups=mesh['fsdp'=4,'x'=2,'core'=2,'tp'=2] {'fsdp','x'}, dimensions={0}, use_global_device_ids=true | all-gather | bytes 589824 | tf_op jit(solution)/shard_map/all_gather | solution.py:171
  184.1 7.8 %copy.86 = bf16[3,4,288,3,128]{4,2,1,0,3:T(8,128)(2,1)} copy(bf16[3,4,288,3,128]{2,3,0,4,1:T(4,128)(2,1)} %bitcast.9) | data formatting | bytes 5308416 | tf_op jit(solution)/shard_map/all_to_all | solution.py:238
  193.8 14.0 %shard_map.254 = (bf16[3,1152,128]{2,1,0:T(8,128)(2,1)S(1)}, f32[3,2,1152]{2,1,0:T(2,128)S(1)}) custom-call(bf16[3,1152,128]{2,1,0:T(8,128)(2,1)S(1)} %get-tuple-element.114.q_ref, bf16[3,1152,128]{2,1,0:T(8,128)(2,1)S(1)} %get-tuple-element.113.k_ref, bf16[3,1152,128]{2,1,0:T(8,128)(2,1)S(1)} %get-tuple-element.112.v_ref, ...), custom_call_target="tpu_custom_call" | custom-call | flops 8153726976 | bytes 3538944 | tf_op jit(solution)/shard_map/pallas_call | solution.py:119
  208.5 6.3 copy.87
  214.7 4.5 all-to-all-start.1
  221.5 13.7 %all-to-all-done.1 = bf16[3,1152,128]{2,0,1:T(4,128)(2,1)} async-done(((bf16[3,1152,128]{2,0,1:T(4,128)(2,1)}), bf16[3,1152,128]{2,0,1:T(4,128)(2,1)}, u32[]{:S(2)}, u32[]{:S(2)}) %all-to-all-start.1) | async-done | bytes 884768 | tf_op jit(solution)/shard_map/all_to_all | solution.py:241
  238.5 2.7 convolution_convert_fusion.3
  249.2 3.2 copy.88
  252.4 29.1 %collective-permute-done.2 = bf16[3,288,1024]{2,1,0:T(8,128)(2,1)S(1)} collective-permute-done((bf16[3,288,1024]{2,1,0:T(8,128)(2,1)S(1)}, bf16[3,288,1024]{2,1,0:T(8,128)(2,1)S(1)}, u32[]{:S(2)}, u32[]{:S(2)}) %collective-permute-start.2) | collective-permute-done | bytes 1769504 | tf_op jit(solution)/shard_map/ppermute | solution.py:162
  283.8 7.1 %multiply_convert_fusion = (bf16[864,2048]{1,0:T(8,128)(2,1)S(1)}, f32[864,2048]{1,0:T(8,128)}) fusion(f32[2048]{0:T(1024)S(1)} %copy-done.39, bf16[864,1024]{1,0:T(8,128)(2,1)S(1)} %bitcast.186, bf16[1024,2048]{1,0:T(8,128)(2,1)S(1)} %bitcast.171), kind=kOutput, calls=%fused_computation.14 | convolution fusion | flops 3641573376 | bytes 16588800 | tf_op jit(solution)/shard_map/dot_general | solution.py:45
  290.9 11.9 %fusion.39 = (f32[2048]{0:T(1024)}, bf16[864,2048]{1,0:T(8,128)(2,1)S(1)}) fusion(f32[864,2048]{1,0:T(8,128)} %get-tuple-element.129, f32[2048]{0:T(1024)S(1)} %copy-done.39, bf16[864,1024]{1,0:T(8,128)(2,1)S(1)} %bitcast.193, bf16[1024,2048]{1,0:T(8,128)(2,1)S(1)} %bitcast.169), kind=kOutput, calls=%fused_computation.111 | convolution fusion | flops 3662804992 | bytes 16596992 | tf_op jit(solution)/shard_map/dot_general | solution.py:45
  302.9 3.9 convolution_convert_fusion.5
  308.3 6.2 convolution_convert_fusion.1
  314.5 5.1 convolution_convert_fusion.4
  319.6 26.4 %collective-permute-done.5 = bf16[3,288,1024]{2,1,0:T(8,128)(2,1)S(1)} collective-permute-done((bf16[3,288,1024]{2,1,0:T(8,128)(2,1)S(1)}, bf16[3,288,1024]{2,1,0:T(8,128)(2,1)S(1)}, u32[]{:S(2)}, u32[]{:S(2)}) %collective-permute-start.5) | collective-permute-done | bytes 1769504 | tf_op jit(solution)/shard_map/ppermute | solution.py:162
  346.0 2.6 multiply_reduce_fusion
  348.6 2.5 fusion.36
  356.6 4.3 all-to-all-start.2
  361.0 9.3 %convert_bitcast_fusion = bf16[1024,2048]{0,1:T(8,128)(2,1)} fusion(bf16[864,2048]{1,0:T(8,128)(2,1)} %copy-done.40, bf16[864,1024]{1,0:T(8,128)(2,1)} %bitcast.192), kind=kOutput, calls=%fused_computation.34 | convolution fusion | flops 3625975808 | bytes 9502720 | tf_op jit(solution)/shard_map/dot_general | solution.py:45
  372.5 8.5 %all-to-all-done.2 = bf16[3,288,512]{1,0,2:T(4,128)(2,1)} async-done(((bf16[3,288,512]{1,0,2:T(4,128)(2,1)}), bf16[3,288,512]{1,0,2:T(4,128)(2,1)}, u32[]{:S(2)}, u32[]{:S(2)}) %all-to-all-start.2) | async-done | bytes 884768 | tf_op jit(solution)/shard_map/all_to_all | solution.py:270
  381.1 2.7 copy.94
  383.8 3.3 dynamic-slice_bitcast_fusion.1
  388.4 3.9 collective-permute-done.9
  394.5 4.5 fusion.16
  399.0 6.7 copy.97
  405.8 3.2 dynamic-slice_bitcast_fusion
  409.1 21.5 %shard_map.255 = (bf16[3,1152,128]{2,1,0:T(8,128)(2,1)S(1)}, bf16[3,1152,128]{2,1,0:T(8,128)(2,1)S(1)}, bf16[3,1152,128]{2,1,0:T(8,128)(2,1)S(1)}) custom-call(bf16[3,1152,128]{2,1,0:T(8,128)(2,1)S(1)} %get-tuple-element.114.q_ref, bf16[3,1152,128]{2,1,0:T(8,128)(2,1)S(1)} %get-tuple-element.113.k_ref, bf16[3,1152,128]{2,1,0:T(8,128)(2,1)S(1)} %get-tuple-element.112.v_ref, ...), custom_call_target="tpu_custom_call" | custom-call | flops 20384317440 | bytes 6193152 | tf_op jit(solution)/shard_map/pallas_call | solution.py:143
  430.9 13.8 %copy.95 = bf16[3,1152,3,128]{3,0,2,1:T(4,128)(2,1)} copy(bf16[3,1152,3,128]{3,1,0,2:T(8,128)(2,1)S(1)} %pad_maximum_fusion.3) | data formatting | bytes 5308416 | tf_op jit(solution)/shard_map/stack | solution.py:276
  444.7 3.7 all-to-all-start.3
  448.5 4.5 fusion.15
  453.1 44.4 %all-to-all-done.3 = bf16[3,1152,3,128]{3,0,2,1:T(4,128)(2,1)S(1)} async-done(((bf16[3,1152,3,128]{3,0,2,1:T(4,128)(2,1)}), bf16[3,1152,3,128]{3,0,2,1:T(4,128)(2,1)S(1)}, u32[]{:S(2)}, u32[]{:S(2)}) %all-to-all-start.3) | async-done | bytes 2654240 | tf_op jit(solution)/shard_map/all_to_all | solution.py:277
  499.3 5.5 convert_reduce_fusion.1
  504.7 2.7 reshape.193
  507.4 5.8 convolution_convert_fusion
  520.4 6.9 %convolution_convert_fusion.2 = bf16[3,288,1024]{2,1,0:T(8,128)(2,1)} fusion(bf16[3,288,1536]{2,1,0:T(8,128)(2,1)} %dot_general.60, bf16[1024,1536,1]{1,0,2:T(8,128)(2,1)} %bitcast.175), kind=kOutput, calls=%fused_computation.71 | convolution fusion | flops 2718793728 | bytes 7569408 | tf_op jit(solution)/shard_map/dot_general | solution.py:45
  527.8 19.3 %all-gather.4 = f32[98304]{0:T(1024)S(1)} all-gather(f32[6144]{0:T(1024)S(1)} %constant_dynamic-update-slice_fusion), channel_id=6, replica_groups=mesh['fsdp'=4,'x'=2,'core'=2,'tp'=2] {'fsdp','x','core'}, dimensions={0}, use_global_device_ids=true | all-gather | bytes 417792 | tf_op jit(solution)/shard_map/all_gather | solution.py:193
  549.8 3.5 fusion.26
  558.1 4.2 add_convert_fusion.1
  562.3 33.3 %collective-permute-done.7 = bf16[3,288,1024]{2,1,0:T(8,128)(2,1)} collective-permute-done((bf16[3,288,1024]{2,1,0:T(8,128)(2,1)}, bf16[3,288,1024]{2,1,0:T(8,128)(2,1)}, u32[]{:S(2)}, u32[]{:S(2)}) %collective-permute-start.7) | collective-permute-done | bytes 1769504 | tf_op jit(solution)/shard_map/ppermute | solution.py:162
  595.6 4.7 fusion.23
  600.4 19.1 %all-gather.3 = f32[49152]{0:T(1024)S(1)} all-gather(f32[3072]{0:T(1024)S(1)} %pad_maximum_fusion.5), channel_id=5, replica_groups=mesh['fsdp'=4,'x'=2,'core'=2,'tp'=2] {'fsdp','x','core'}, dimensions={0}, use_global_device_ids=true | all-gather | bytes 208896 | tf_op jit(solution)/shard_map/all_gather | solution.py:193
  620.7 5.1 fusion.22
  629.4 38.9 %reduce-scatter.5.cloned.1.call-done = bf16[64,1536]{1,0:T(8,128)(2,1)} async-done(((bf16[512,1536]{1,0:T(8,128)(2,1)}), bf16[64,1536]{1,0:T(8,128)(2,1)}) %reduce-scatter.5.cloned.1.call-update) | async-done | bytes 196624 | tf_op jit(solution)/shard_map/reduce_scatter | solution.py:188
  (186 shorter events, 67.8 us)
Async XLA Ops:
  7.2 53.3 %copy-start.4 = (bf16[3,288,1024]{2,1,0:T(8,128)(2,1)S(1)}, bf16[3,288,1024]{2,1,0:T(8,128)(2,1)}, u32[]{:S(2)}) copy-start(bf16[3,288,1024]{2,1,0:T(8,128)(2,1)} %param.15) | copy-start | bytes 5308420
  7.2 54.0 %copy-start.27 = (f32[1024]{0:T(1024)S(1)}, f32[1024]{0:T(1024)}, u32[]{:S(2)}) copy-start(f32[1024]{0:T(1024)} %param.17) | copy-start | bytes 12292
  7.2 54.0 %copy-start.38 = (f32[1024]{0:T(1024)S(1)}, f32[1024]{0:T(1024)}, u32[]{:S(2)}) copy-start(f32[1024]{0:T(1024)} %param.18) | copy-start | bytes 12292
  7.2 50.5 %all-gather.9.cloned.1.call-start = ((), (), s32[]{:S(2)}) async-start(), calls=%async_computation.8 | async-start | bytes 1769472 | tf_op jit(solution)/shard_map/all_gather | solution.py:171
  9.4 174.0 %all-gather.11.cloned.1.call-start = ((), (), s32[]{:S(2)}) async-start(), calls=%async_computation.13 | async-start | bytes 2359296 | tf_op jit(solution)/shard_map/all_gather | solution.py:171
  10.2 173.8 %all-gather.13.cloned.1.call-start = ((), (), s32[]{:S(2)}) async-start(), calls=%async_computation.14 | async-start | bytes 2359296 | tf_op jit(solution)/shard_map/all_gather | solution.py:171
  57.7 4.2 collective-permute-start
  58.5 3.4 copy-start.17
  81.7 5.1 copy-start.26
  81.7 99.6 %copy-start.25 = (s32[3,1152]{1,0:T(4,128)S(1)}, s32[3,1152]{1,0:T(4,128)}, u32[]{:S(2)}) copy-start(s32[3,1152]{1,0:T(4,128)} %param.16) | copy-start | bytes 41476
  81.7 102.5 %all-to-all-start = ((bf16[3,288,3,512]{1,2,0,3:T(4,128)(2,1)}), bf16[3,288,3,512]{1,2,0,3:T(4,128)(2,1)}, u32[]{:S(2)}, u32[]{:S(2)}) async-start(bf16[3,288,3,512]{1,2,0,3:T(4,128)(2,1)} %copy.84), calls=%async_computation | async-start | bytes 9437184 | tf_op jit(solution)/shard_map/all_to_all | solution.py:238
  181.3 38.0 %collective-permute-start.1 = (bf16[8,64,512]{2,1,0:T(8,128)(2,1)S(1)}, bf16[8,64,512]{2,1,0:T(8,128)(2,1)}, u32[]{:S(2)}, u32[]{:S(2)}) collective-permute-start(bf16[8,64,512]{2,1,0:T(8,128)(2,1)S(1)} %bitcast.178), channel_id=1, source_target_pairs={{0,2},{2,0},{1,3},{3,1},{4,6},{6,4},{5,7},{7,5},{8,10},{10,8},{9,1... | collective-permute-start | bytes 1572872 | tf_op jit(solution)/shard_map/ppermute | solution.py:162
  183.5 59.4 %collective-permute-start.3 = (bf16[8,64,2048]{2,1,0:T(8,128)(2,1)}, bf16[8,64,2048]{2,1,0:T(8,128)(2,1)}, u32[]{:S(2)}, u32[]{:S(2)}) collective-permute-start(bf16[8,64,2048]{2,1,0:T(8,128)(2,1)} %bitcast.182), channel_id=1, source_target_pairs={{0,2},{2,0},{1,3},{3,1},{4,6},{6,4},{5,7},{7,5},{8,10},{10,8},{9,1... | collective-permute-start | bytes 6291464 | tf_op jit(solution)/shard_map/ppermute | solution.py:162
  184.0 61.6 %collective-permute-start.4 = (bf16[8,64,2048]{2,1,0:T(8,128)(2,1)}, bf16[8,64,2048]{2,1,0:T(8,128)(2,1)}, u32[]{:S(2)}, u32[]{:S(2)}) collective-permute-start(bf16[8,64,2048]{2,1,0:T(8,128)(2,1)} %bitcast.184), channel_id=1, source_target_pairs={{0,2},{2,0},{1,3},{3,1},{4,6},{6,4},{5,7},{7,5},{8,10},{10,8},{9,1... | collective-permute-start | bytes 6291464 | tf_op jit(solution)/shard_map/ppermute | solution.py:162
  214.7 20.4 %all-to-all-start.1 = ((bf16[3,1152,128]{2,0,1:T(4,128)(2,1)}), bf16[3,1152,128]{2,0,1:T(4,128)(2,1)}, u32[]{:S(2)}, u32[]{:S(2)}) async-start(bf16[3,1152,128]{2,0,1:T(4,128)(2,1)} %copy.87), calls=%async_computation.1 | async-start | bytes 2359296 | tf_op jit(solution)/shard_map/all_to_all | solution.py:241
  238.5 4.3 copy-start.11
  241.3 40.2 %collective-permute-start.2 = (bf16[3,288,1024]{2,1,0:T(8,128)(2,1)S(1)}, bf16[3,288,1024]{2,1,0:T(8,128)(2,1)S(1)}, u32[]{:S(2)}, u32[]{:S(2)}) collective-permute-start(bf16[3,288,1024]{2,1,0:T(8,128)(2,1)S(1)} %convolution_convert_fusion.3), channel_id=1, source_target_pairs={{0,1},{1,0},{2,3},{3,2},{4,5},{5,4},{6,7},{7,6},{8,9},{9,8},{10,11... | collective-permute-start | bytes 5308424 | tf_op jit(solution)/shard_map/ppermute | solution.py:162
  248.8 32.7 %copy-start.5 = (bf16[3,288,1024]{2,1,0:T(8,128)(2,1)S(1)}, bf16[3,288,1024]{2,1,0:T(8,128)(2,1)}, u32[]{:S(2)}) copy-start(bf16[3,288,1024]{2,1,0:T(8,128)(2,1)} %param.15) | copy-start | bytes 5308420
  248.8 32.6 %copy-start.36 = (f32[1024]{0:T(1024)S(1)}, f32[1024]{0:T(1024)}, u32[]{:S(2)}) copy-start(f32[1024]{0:T(1024)} %param.22) | copy-start | bytes 12292
  282.4 66.2 %copy-start.2 = (f32[3,288,1024]{2,1,0:T(8,128)}, f32[3,288,1024]{2,1,0:T(8,128)S(1)}, u32[]{:S(2)}) copy-start(f32[3,288,1024]{2,1,0:T(8,128)S(1)} %get-tuple-element.103) | copy-start | bytes 10616836
  283.8 7.1 %copy-start.16 = (bf16[3,288,1024]{2,1,0:T(8,128)(2,1)S(1)}, bf16[3,288,1024]{2,1,0:T(8,128)(2,1)}, u32[]{:S(2)}) copy-start(bf16[3,288,1024]{2,1,0:T(8,128)(2,1)} %param.29) | copy-start | bytes 5308420
  290.9 23.6 %copy-start.40 = (bf16[864,2048]{1,0:T(8,128)(2,1)}, bf16[864,2048]{1,0:T(8,128)(2,1)S(1)}, u32[]{:S(2)}) copy-start(bf16[864,2048]{1,0:T(8,128)(2,1)S(1)} %get-tuple-element.128) | copy-start | bytes 10616836
  306.7 39.3 %collective-permute-start.5 = (bf16[3,288,1024]{2,1,0:T(8,128)(2,1)S(1)}, bf16[3,288,1024]{2,1,0:T(8,128)(2,1)S(1)}, u32[]{:S(2)}, u32[]{:S(2)}) collective-permute-start(bf16[3,288,1024]{2,1,0:T(8,128)(2,1)S(1)} %convolution_convert_fusion.5), channel_id=1, source_target_pairs={{0,1},{1,0},{2,3},{3,2},{4,5},{5,4},{6,7},{7,6},{8,9},{9,8},{10,11... | collective-permute-start | bytes 5308424 | tf_op jit(solution)/shard_map/ppermute | solution.py:162
  356.6 24.5 %all-to-all-start.2 = ((bf16[3,288,512]{1,0,2:T(4,128)(2,1)}), bf16[3,288,512]{1,0,2:T(4,128)(2,1)}, u32[]{:S(2)}, u32[]{:S(2)}) async-start(bf16[3,288,512]{1,0,2:T(4,128)(2,1)} %copy.92), calls=%async_computation.2 | async-start | bytes 3145728 | tf_op jit(solution)/shard_map/all_to_all | solution.py:270
  360.9 9.4 %copy-start.20 = (bf16[3,4,288,128]{3,1,2,0:T(4,128)(2,1)S(1)}, bf16[3,4,288,128]{3,1,2,0:T(4,128)(2,1)}, u32[]{:S(2)}) copy-start(bf16[3,4,288,128]{3,1,2,0:T(4,128)(2,1)} %copy.88) | copy-start | bytes 2654212
  360.9 195.0 %reduce-scatter.7.cloned.1.call-start = ((), (), s32[]{:S(2)}) async-start(), calls=%async_computation.10 | async-start | bytes 589824 | tf_op jit(solution)/shard_map/reduce_scatter | solution.py:188
  361.0 9.3 %copy-start.15 = (bf16[3,288,1024]{2,1,0:T(8,128)(2,1)S(1)}, bf16[3,288,1024]{2,1,0:T(8,128)(2,1)}, u32[]{:S(2)}) copy-start(bf16[3,288,1024]{2,1,0:T(8,128)(2,1)} %copy-done.14) | copy-start | bytes 5308420
  387.1 7.5 %collective-permute-start.10 = (bf16[8,64,2048]{2,1,0:T(8,128)(2,1)}, bf16[8,64,2048]{2,1,0:T(8,128)(2,1)}, u32[]{:S(2)}, u32[]{:S(2)}) collective-permute-start(bf16[8,64,2048]{2,1,0:T(8,128)(2,1)} %dynamic-slice_bitcast_fusion.1), channel_id=1, source_target_pairs={{0,2},{2,0},{1,3},{3,1},{4,6},{6,4},{5,7},{7,5},{8,10},{10,8},{9,1... | collective-permute-start | bytes 6291464 | tf_op jit(solution)/shard_map/ppermute | solution.py:162
  387.9 4.4 collective-permute-start.9
  394.5 231.3 %reduce-scatter.9.cloned.1.call-start = ((), (), s32[]{:S(2)}) async-start(), calls=%async_computation.11 | async-start | bytes 2359296 | tf_op jit(solution)/shard_map/reduce_scatter | solution.py:188
  409.0 39.6 %collective-permute-start.11 = (bf16[8,64,2048]{2,1,0:T(8,128)(2,1)}, bf16[8,64,2048]{2,1,0:T(8,128)(2,1)}, u32[]{:S(2)}, u32[]{:S(2)}) collective-permute-start(bf16[8,64,2048]{2,1,0:T(8,128)(2,1)} %dynamic-slice_bitcast_fusion), channel_id=1, source_target_pairs={{0,2},{2,0},{1,3},{3,1},{4,6},{6,4},{5,7},{7,5},{8,10},{10,8},{9,1... | collective-permute-start | bytes 6291464 | tf_op jit(solution)/shard_map/ppermute | solution.py:162
  444.7 52.8 %all-to-all-start.3 = ((bf16[3,1152,3,128]{3,0,2,1:T(4,128)(2,1)}), bf16[3,1152,3,128]{3,0,2,1:T(4,128)(2,1)S(1)}, u32[]{:S(2)}, u32[]{:S(2)}) async-start(bf16[3,1152,3,128]{3,0,2,1:T(4,128)(2,1)} %copy.95), calls=%async_computation.3 | async-start | bytes 7077888 | tf_op jit(solution)/shard_map/all_to_all | solution.py:277
  448.5 179.1 %reduce-scatter.11.cloned.1.call-start = ((), (), s32[]{:S(2)}) async-start(), calls=%async_computation.12 | async-start | bytes 2359296 | tf_op jit(solution)/shard_map/reduce_scatter | solution.py:188
  453.0 215.3 %reduce-scatter.5.cloned.1.call-start = ((), (), s32[]{:S(2)}) async-start(), calls=%async_computation.9 | async-start | bytes 1769472 | tf_op jit(solution)/shard_map/reduce_scatter | solution.py:188
  507.4 8.9 %copy-start.35 = (f32[2048]{0:T(1024)S(1)}, f32[2048]{0:T(1024)}, u32[]{:S(2)}) copy-start(f32[2048]{0:T(1024)} %get-tuple-element.104) | copy-start | bytes 24580
  507.4 8.9 %copy-start.34 = (f32[1024]{0:T(1024)S(1)}, f32[1024]{0:T(1024)}, u32[]{:S(2)}) copy-start(f32[1024]{0:T(1024)} %get-tuple-element.115) | copy-start | bytes 12292
  507.4 8.9 %copy-start.33 = (f32[1024]{0:T(1024)S(1)}, f32[1024]{0:T(1024)}, u32[]{:S(2)}) copy-start(f32[1024]{0:T(1024)} %get-tuple-element.98) | copy-start | bytes 12292
  516.3 33.5 %collective-permute-start.8 = (bf16[8,64,1536]{2,1,0:T(8,128)(2,1)}, bf16[8,64,1536]{2,1,0:T(8,128)(2,1)}, u32[]{:S(2)}, u32[]{:S(2)}) collective-permute-start(bf16[8,64,1536]{2,1,0:T(8,128)(2,1)} %dynamic-slice_bitcast_fusion.2), channel_id=1, source_target_pairs={{0,2},{2,0},{1,3},{3,1},{4,6},{6,4},{5,7},{7,5},{8,10},{10,8},{9,1... | collective-permute-start | bytes 4718600 | tf_op jit(solution)/shard_map/ppermute | solution.py:162
  516.3 41.8 %collective-permute-start.6 = (bf16[3,288,1024]{2,1,0:T(8,128)(2,1)}, bf16[3,288,1024]{2,1,0:T(8,128)(2,1)}, u32[]{:S(2)}, u32[]{:S(2)}) collective-permute-start(bf16[3,288,1024]{2,1,0:T(8,128)(2,1)} %convolution_convert_fusion.4), channel_id=1, source_target_pairs={{0,1},{1,0},{2,3},{3,2},{4,5},{5,4},{6,7},{7,6},{8,9},{9,8},{10,11... | collective-permute-start | bytes 5308424 | tf_op jit(solution)/shard_map/ppermute | solution.py:162
  520.4 7.4 %copy-start.32 = (f32[1024]{0:T(1024)S(1)}, f32[1024]{0:T(1024)}, u32[]{:S(2)}) copy-start(f32[1024]{0:T(1024)} %get-tuple-element.90) | copy-start | bytes 12292
  520.4 7.4 %copy-start.31 = (f32[1024]{0:T(1024)S(1)}, f32[1024]{0:T(1024)}, u32[]{:S(2)}) copy-start(f32[1024]{0:T(1024)} %get-tuple-element.96) | copy-start | bytes 12292
  527.3 68.3 %collective-permute-start.7 = (bf16[3,288,1024]{2,1,0:T(8,128)(2,1)}, bf16[3,288,1024]{2,1,0:T(8,128)(2,1)}, u32[]{:S(2)}, u32[]{:S(2)}) collective-permute-start(bf16[3,288,1024]{2,1,0:T(8,128)(2,1)} %convolution_convert_fusion.2), channel_id=1, source_target_pairs={{0,1},{1,0},{2,3},{3,2},{4,5},{5,4},{6,7},{7,6},{8,9},{9,8},{10,11... | collective-permute-start | bytes 5308424 | tf_op jit(solution)/shard_map/ppermute | solution.py:162
  547.9 10.2 %copy-start.3 = (f32[3,288,1024]{2,1,0:T(8,128)S(1)}, f32[3,288,1024]{2,1,0:T(8,128)}, u32[]{:S(2)}) copy-start(f32[3,288,1024]{2,1,0:T(8,128)} %copy-done.2) | copy-start | bytes 10616836
  557.5 4.8 copy-start.30
  557.5 38.1 %copy-start.22 = (f32[3,288]{1,0:T(4,128)S(1)}, f32[3,288]{1,0:T(4,128)}, u32[]{:S(2)}) copy-start(f32[3,288]{1,0:T(4,128)} %copy-done.21) | copy-start | bytes 10372
  557.5 38.1 %copy-start.24 = (f32[3,288]{1,0:T(4,128)S(1)}, f32[3,288]{1,0:T(4,128)}, u32[]{:S(2)}) copy-start(f32[3,288]{1,0:T(4,128)} %copy-done.23) | copy-start | bytes 10372
  562.3 58.4 %copy-start.6 = (bf16[3,288,1024]{2,1,0:T(8,128)(2,1)S(1)}, bf16[3,288,1024]{2,1,0:T(8,128)(2,1)}, u32[]{:S(2)}) copy-start(bf16[3,288,1024]{2,1,0:T(8,128)(2,1)} %param.15) | copy-start | bytes 5308420
  562.3 58.4 %copy-start.28 = (f32[1024]{0:T(1024)S(1)}, f32[1024]{0:T(1024)}, u32[]{:S(2)}) copy-start(f32[1024]{0:T(1024)} %param.17) | copy-start | bytes 12292
  (16 other events, 27.4 us)
Sparse Core Ops, SparseCore 0:
  10.8 46.8 all-gather.8
  59.8 56.3 all-gather.10
  118.4 62.6 all-gather.12
  394.6 60.4 reduce-scatter.6
  458.9 71.4 reduce-scatter.8
  534.1 66.2 reduce-scatter.10
  604.3 63.9 reduce-scatter.4

commit v2 on v1

--- a/solution.py
+++ b/solution.py
@@ -61,27 +61,37 @@
     return jnp.where(allowed, scores, MASKED)
 
 
-def forward_kernel(q_ref, k_ref, v_ref, start_ref, out_ref, lse_ref):
-    seq_len, width = q_ref.shape[1:]
+def forward_kernel(qkv_ref, start_ref, out_ref, lse_ref, out):
+    parts, _, local_len, triple = qkv_ref.shape
+    seq_len, width = parts * local_len, triple // 3
     block = query_block(seq_len)
+    qkv = qkv_ref[...].reshape(seq_len, triple)
     for first in range(0, seq_len, block):
         rows = slice(first, first + block)
         keys = slice(0, first + block)
         start = start_ref[0, :, rows]
         for head in range(width // HD):
-            cols = slice(head * HD, (head + 1) * HD)
-            scores = masked_scores(k_ref[0, keys, cols], q_ref[0, rows, cols], start, first)
+            at = head * HD
+            q, k, v = (
+                qkv[span, j * width + at : j * width + at + HD]
+                for j, span in enumerate((rows, keys, keys))
+            )
+            scores = masked_scores(k, q, start, first)
             highest = jnp.max(scores, 0, keepdims=True)
             raised = jnp.exp2(scores - highest)
             summed = jnp.sum(raised, 0, keepdims=True)
             probs = (raised * (1.0 / summed)).astype(BF)
-            out_ref[0, rows, cols] = dot(probs, v_ref[0, keys, cols], 0, 0).astype(BF)
+            out[rows, at : at + HD] = dot(probs, v, 0, 0).astype(BF)
             lse_ref[0, head : head + 1, rows] = highest + jnp.log2(summed)
-
-
-def backward_kernel(q_ref, k_ref, v_ref, start_ref, lse_ref, g_ref, dq_ref, dk_ref, dv_ref, ak, av):
-    seq_len, width = q_ref.shape[1:]
+    out_ref[...] = out[...].reshape(out_ref.shape)
+
+
+def backward_kernel(qkv_ref, start_ref, lse_ref, g_ref, out_ref, out, ak, av):
+    parts, _, local_len, triple = qkv_ref.shape
+    seq_len, width = parts * local_len, triple // 3
     block = query_block(seq_len)
+    qkv = qkv_ref[...].reshape(seq_len, triple)
+    grads = g_ref[...].reshape(seq_len, width)
     ak[...] = jnp.zeros_like(ak)
     av[...] = jnp.zeros_like(av)
     for first in range(0, seq_len, block):
@@ -89,64 +99,74 @@
         keys = slice(0, first + block)
         start = start_ref[0, :, rows]
         for head in range(width // HD):
-            cols = slice(head * HD, (head + 1) * HD)
-            k, q, g = k_ref[0, keys, cols], q_ref[0, rows, cols], g_ref[0, rows, cols]
+            at = head * HD
+            q, k, v = (
+                qkv[span, j * width + at : j * width + at + HD]
+                for j, span in enumerate((rows, keys, keys))
+            )
+            g = grads[rows, at : at + HD]
             scores = masked_scores(k, q, start, first)
             probs = jnp.exp2(scores - lse_ref[0, head : head + 1, rows])
-            grad_probs = dot(v_ref[0, keys, cols], g, 1, 1)
+            grad_probs = dot(v, g, 1, 1)
             row_dot = jnp.sum(probs * grad_probs, 0, keepdims=True)
             grad_scores = (probs * (grad_probs - row_dot)).astype(BF)
-            dq_ref[0, rows, cols] = (dot(grad_scores, k, 0, 0) * HD ** (-0.5)).astype(BF)
+            out[rows, at : at + HD] = (dot(grad_scores, k, 0, 0) * HD ** (-0.5)).astype(BF)
             ak[head, keys, :] += dot(grad_scores, q, 1, 0)
             av[head, keys, :] += dot(probs.astype(BF), g, 1, 0)
     for head in range(width // HD):
-        cols = slice(head * HD, (head + 1) * HD)
-        dk_ref[0, :, cols] = (ak[head] * HD ** (-0.5)).astype(BF)
-        dv_ref[0, :, cols] = av[head].astype(BF)
-
-
-def part_spec(seq_len, width, part):
-    return pl.BlockSpec((1, seq_len, width), lambda s: (s, 0, part))
-
-
-def attend_forward(q, k, v, start):
-    seqs, seq_len, width = q.shape
+        at = width + head * HD
+        out[:, at : at + HD] = (ak[head] * HD ** (-0.5)).astype(BF)
+        out[:, at + width : at + width + HD] = av[head].astype(BF)
+    out_ref[...] = out[...].reshape(out_ref.shape)
+
+
+def attend_forward(qkv, start):
+    parts, seqs, local_len, triple = qkv.shape
+    seq_len, width = parts * local_len, triple // 3
     heads = width // HD
-    whole = pl.BlockSpec((1, seq_len, width), lambda s: (s, 0, 0))
-    row = pl.BlockSpec((1, 1, seq_len), lambda s: (s, 0, 0))
-    lse = pl.BlockSpec((1, heads, seq_len), lambda s: (s, 0, 0))
     square = seqs * heads * seq_len * seq_len
     return pl.pallas_call(
         forward_kernel,
         grid=(seqs,),
-        in_specs=[whole, whole, whole, row],
-        out_specs=[whole, lse],
+        in_specs=[
+            pl.BlockSpec((parts, 1, local_len, triple), lambda s: (0, s, 0, 0)),
+            pl.BlockSpec((1, 1, seq_len), lambda s: (s, 0, 0)),
+        ],
+        out_specs=[
+            pl.BlockSpec((parts, 1, local_len, width), lambda s: (0, s, 0, 0)),
+            pl.BlockSpec((1, heads, seq_len), lambda s: (s, 0, 0)),
+        ],
         out_shape=[
-            jax.ShapeDtypeStruct((seqs, seq_len, width), BF),
+            jax.ShapeDtypeStruct((parts, seqs, local_len, width), BF),
             jax.ShapeDtypeStruct((seqs, heads, seq_len), F32),
         ],
+        scratch_shapes=[pltpu.VMEM((seq_len, width), BF)],
         compiler_params=pltpu.CompilerParams(vmem_limit_bytes=40 * 1024 * 1024),
         cost_estimate=pl.CostEstimate(
             flops=square * HD * 16, bytes_accessed=seqs * seq_len * width * 8, transcendentals=square
         ),
-    )(q, k, v, start)
-
-
-def attend_backward(q, k, v, start, lses, grads):
-    seqs, seq_len, width = q.shape
+    )(qkv, start)
+
+
+def attend_backward(qkv, start, lses, grads):
+    parts, seqs, local_len, triple = qkv.shape
+    seq_len, width = parts * local_len, triple // 3
     heads = width // HD
-    whole = pl.BlockSpec((1, seq_len, width), lambda s: (s, 0, 0))
-    row = pl.BlockSpec((1, 1, seq_len), lambda s: (s, 0, 0))
-    lse = pl.BlockSpec((1, heads, seq_len), lambda s: (s, 0, 0))
     square = seqs * heads * seq_len * seq_len
-    shape = jax.ShapeDtypeStruct((seqs, seq_len, width), BF)
+    wide = pl.BlockSpec((parts, 1, local_len, triple), lambda s: (0, s, 0, 0))
     return pl.pallas_call(
         backward_kernel,
         grid=(seqs,),
-        in_specs=[whole, whole, whole, row, lse, whole],
-        out_specs=[whole, whole, whole],
-        out_shape=[shape, shape, shape],
+        in_specs=[
+            wide,
+            pl.BlockSpec((1, 1, seq_len), lambda s: (s, 0, 0)),
+            pl.BlockSpec((1, heads, seq_len), lambda s: (s, 0, 0)),
+            pl.BlockSpec((parts, 1, local_len, width), lambda s: (0, s, 0, 0)),
+        ],
+        out_specs=wide,
+        out_shape=jax.ShapeDtypeStruct(qkv.shape, BF),
         scratch_shapes=[
+            pltpu.VMEM((seq_len, triple), BF),
             pltpu.VMEM((heads, seq_len, HD), F32),
             pltpu.VMEM((heads, seq_len, HD), F32),
         ],
@@ -154,12 +174,24 @@
         cost_estimate=pl.CostEstimate(
             flops=square * HD * 40, bytes_accessed=seqs * seq_len * width * 14, transcendentals=square
         ),
-    )(q, k, v, start, lses, grads)
+    )(qkv, start, lses, grads)
 
 
 def swap(values, axis):
     count = lax.axis_size(axis)
     return lax.ppermute(values, axis, [(i, i ^ 1) for i in range(count)])
+
+
+def trade(values):
+    return lax.all_to_all(values, CTX, split_axis=0, concat_axis=0, tiled=True)
+
+
+def by_part(values, parts):
+    return values.reshape(values.shape[0], parts, -1).transpose(1, 0, 2)
+
+
+def by_row(values):
+    return values.transpose(1, 0, 2).reshape(values.shape[1], -1)
 
 
 def pair_sum(values):
@@ -176,7 +208,7 @@
     return jnp.stack([low, high], axis=1).reshape(-1, shard.shape[1])
 
 
-def scatter_rows(grad):
+def core_sum(grad):
     groups = lax.axis_size("fsdp") * lax.axis_size("x")
     rows = grad.shape[0] // (2 * groups)
     core = lax.axis_index("core")
@@ -184,13 +216,23 @@
     mine = lax.dynamic_index_in_dim(halves, core, 1, keepdims=False)
     theirs = lax.dynamic_index_in_dim(halves, 1 - core, 1, keepdims=False)
     summed = (mine.astype(F32) + swap(theirs, "core").astype(F32)).astype(BF)
-    summed = summed.reshape(groups * rows, grad.shape[1])
+    return summed.reshape(groups * rows, grad.shape[1])
+
+
+def scatter_rows(summed):
     return lax.psum_scatter(summed, SAME, scatter_dimension=0, tiled=True).astype(F32)
 
 
 def small_sums(*vectors):
     flat = jnp.concatenate([v.reshape(-1) for v in vectors])
-    total = jnp.sum(lax.all_gather(flat, ALL, axis=0, tiled=False), 0)
+    total = flat
+    for axis in ALL:
+        count = lax.axis_size(axis)
+        step = 1
+        while step < count:
+            pairs = [(i, i ^ step) for i in range(count)]
+            total = total + lax.ppermute(total, axis, pairs)
+            step *= 2
     outs, at = [], 0
     for v in vectors:
         outs.append(total[at : at + v.size].reshape(v.shape))
@@ -220,11 +262,16 @@
     heads_cols = qkv_weight.shape[2]
     rows = seqs * local_len
     barrier = lax.optimization_barrier
-    qkv_rows = jnp.moveaxis(qkv_weight, 0, 1).reshape(qkv_weight.shape[1], 3 * heads_cols)
-    w_qkv = gather_rows(qkv_rows)
-    w_out = gather_rows(out_weight.T)
-    w_up = gather_rows(up_weight)
-    w_down = gather_rows(down_weight.T)
+    parts = lax.axis_size("x") * lax.axis_size("core")
+    shard = qkv_weight.shape[1]
+    width = heads_cols // parts
+    qkv_rows = qkv_weight.reshape(3, shard, parts, width).transpose(1, 2, 0, 3)
+    qkv_rows = qkv_rows.reshape(shard, 3 * heads_cols)
+    first_set = gather_rows(jnp.concatenate([qkv_rows, out_weight.T], 1))
+    w_qkv, w_out = first_set[:, : 3 * heads_cols], first_set[:, 3 * heads_cols :]
+    units = up_weight.shape[1]
+    second_set = gather_rows(jnp.concatenate([up_weight, down_weight.T], 1))
+    w_up, w_down = second_set[:, :units], second_set[:, units:]
 
     start = jnp.sum(
         (segment_ids[:, None, :] < segment_ids[:, :, None]).astype(jnp.int32), -1
@@ -232,14 +279,12 @@
     inputs = tokens.astype(F32)
     normed_in, normed_one, inverse_one = norm_forward(inputs, first_gain, first_shift)
     first_in = normed_in.astype(BF)
-    bias_row = jnp.concatenate([qv_bias[0], jnp.zeros_like(qv_bias[0]), qv_bias[1]])
+    bias_row = jnp.stack([qv_bias[0], jnp.zeros_like(qv_bias[0]), qv_bias[1]])
+    bias_row = bias_row.reshape(3, parts, width).transpose(1, 0, 2).reshape(-1)
     projected = (dot(first_in.reshape(rows, model), w_qkv, 1, 0) + bias_row).astype(BF)
-    projected = projected.reshape(seqs, local_len, 3, heads_cols)
-    by_heads = lax.all_to_all(projected, CTX, split_axis=3, concat_axis=1, tiled=True)
-    q, k, v = by_heads[:, :, 0], by_heads[:, :, 1], by_heads[:, :, 2]
-    attended, lses = attend_forward(q, k, v, start)
-    mixed = lax.all_to_all(attended, CTX, split_axis=1, concat_axis=2, tiled=True)
-    mixed_rows = mixed.reshape(rows, heads_cols)
+    qkv = trade(by_part(projected, parts)).reshape(parts, seqs, local_len, 3 * width)
+    attended, lses = attend_forward(qkv, start)
+    mixed_rows = by_row(trade(attended.reshape(parts, rows, width)))
 
     attn_part = dot(mixed_rows, w_out, 1, 1).reshape(seqs, local_len, model)
     cot_rows = cotangent.reshape(rows, model)
@@ -260,36 +305,38 @@
     )
     grad_mid = grad_top + grad_mid_norm
     grad_mid_low = grad_mid.astype(BF).reshape(rows, model)
-    grad_mixed = dot(grad_mid_low, w_out, 1, 0).astype(BF).reshape(seqs, local_len, heads_cols)
+    grad_mixed = by_part(dot(grad_mid_low, w_out, 1, 0).astype(BF), parts)
 
     grad_down = dot(cot_rows, hidden, 0, 0).astype(BF)
     grad_up = dot(second_in, grad_pre_low, 0, 0).astype(BF)
     grad_out = dot(grad_mid_low, mixed_rows, 0, 0).astype(BF)
     down_part = dot(hidden, w_down, 1, 1).reshape(seqs, local_len, model)
 
-    grad_att = lax.all_to_all(grad_mixed, CTX, split_axis=2, concat_axis=1, tiled=True)
-    grad_att, grad_down, grad_up, grad_out, down_part = barrier(
-        (grad_att, grad_down, grad_up, grad_out, down_part.astype(BF))
-    )
+    grad_att = trade(grad_mixed).reshape(parts, seqs, local_len, width)
+    early = jnp.concatenate([grad_down, grad_up, grad_out], 1)
+    grad_att, early, down_part = barrier((grad_att, core_sum(early), down_part.astype(BF)))
+    own_early = scatter_rows(early)
     layer_out = (middle + pair_sum(down_part) + down_bias).astype(BF)
-    dq, dk, dv = attend_backward(q, k, v, start, lses, grad_att)
-    grad_heads = jnp.stack([dq, dk, dv], axis=2)
-    grad_proj = lax.all_to_all(grad_heads, CTX, split_axis=1, concat_axis=3, tiled=True)
-    grad_proj = grad_proj.reshape(rows, 3 * heads_cols)
+    grad_heads = attend_backward(qkv, start, lses, grad_att)
+    grad_proj = by_row(trade(grad_heads.reshape(parts, rows, 3 * width)))
     grad_one_part = dot(grad_proj, w_qkv, 1, 1).reshape(seqs, local_len, model)
-    grad_one_sum = pair_sum(grad_one_part)
     grad_qkv = dot(first_in.reshape(rows, model), grad_proj, 0, 0)
+    sent = grad_one_part.astype(BF)
+    received, own_early, late = barrier((swap(sent, "tp"), own_early, core_sum(grad_qkv)))
+    grad_one_sum = sent.astype(F32) + received.astype(F32)
     grad_in_norm, grad_gain_one, grad_shift_one = norm_backward(
         grad_one_sum, normed_one, inverse_one, first_gain
     )
     grad_inputs = grad_mid + grad_in_norm
 
-    own_down = scatter_rows(grad_down).T
-    own_up = scatter_rows(grad_up)
-    own_out = scatter_rows(grad_out).T
-    own_qkv = scatter_rows(grad_qkv)
-    own_qkv = jnp.moveaxis(own_qkv.reshape(-1, 3, heads_cols), 1, 0)
-    grad_qv_b = jnp.sum(grad_proj.astype(F32), axis=0).reshape(3, heads_cols)[0::2]
+    own_down = own_early[:, :units].T
+    own_up = own_early[:, units : 2 * units]
+    own_out = own_early[:, 2 * units :].T
+    own_qkv = scatter_rows(late)
+    own_qkv = own_qkv.reshape(shard, parts, 3, width).transpose(2, 0, 1, 3)
+    own_qkv = own_qkv.reshape(3, shard, heads_cols)
+    grad_qv_b = jnp.sum(grad_proj.astype(F32), axis=0).reshape(parts, 3, width)
+    grad_qv_b = grad_qv_b.transpose(1, 0, 2).reshape(3, heads_cols)[0::2]
     sum_up_b, sum_down_b, sum_out_b, sum_gain_two, sum_shift_two = small_sums(
         grad_up_b,
         jnp.sum(grad_top, axis=(0, 1)),

time: 683 us -> 573 us (0.84)
  blocking collectives: 133 us -> 48.7 us
  local copies, waits for them, and re-layouts: 94.3 us -> 52.8 us
  other arithmetic: 61.7 us -> 76.4 us
    all_gather x3 -> x0, blocking collectives: 133 us -> none  [the longest x1 94.5 us: gather_rows(): part = lax.all_gather(shard, SAME, axis=0, tiled=False)]
    all_to_all x0 -> x1, blocking collectives: none -> 48.7 us  [trade(): return lax.all_to_all(values, CTX, split_axis=0, concat_axis=0, tiled=True)]
    reduce_scatter x4 -> x2, waiting for transfers between devices: 39 us -> 0.2 us  [scatter_rows(): lax.psum_scatter(summed, SAME, scatter_dimension=0, tiled=True).astype(F32)]
    ppermute x12 -> x8, waiting for transfers between devices: 93.3 us -> 119 us  [swap(): return lax.ppermute(values, axis, [(i, i ^ 1) for i in range(count)])]
    concatenate x1 -> x3, other arithmetic: 0.01 us -> 23.2 us  [the longest x1 19.8 us: local(): early = jnp.concatenate([grad_down, grad_up, grad_out], 1)]
    ppermute x0 -> x8, waiting for transfers between devices: none -> 21.7 us  [small_sums(): total = total + lax.ppermute(total, axis, pairs)]
    all_to_all x4 -> x0, local copies, waits for them, and re-layouts: 15.8 us -> none  [the longest x1 7.81 us: local(): lax.all_to_all(projected, CTX, split_axis=3, concat_axis=1, tiled=True)]
    another operation x4 -> x1, local copies, waits for them, and re-layouts: 15.4 us -> 0.07 us  [local(): bias_row = jnp.stack([qv_bias[0], jnp.zeros_like(qv_bias[0]), qv_bias[1]])]
  transfers between devices with their start and end apart: 23 -> 23, of which waited for: 10 -> 18; matrix products, arithmetic and copies ran while one was open for 25% -> 19% of each run, Pallas kernels for 5% -> 7%
where the time goes in v2:
time: 573 us; the launch traced here: 564 us
  waiting for transfers between devices  250 us (44%)
  other arithmetic  76.4 us (13%)
  matrix products  64.3 us (11%)
  local copies, waits for them, and re-layouts  52.8 us (9%)
  blocking collectives  48.7 us (8%)
  Pallas kernels  37.8 us (7%)
  starting transfers between devices  19.4 us (3%)
  between operations  14.9 us (3%)
    ppermute x8, waiting for transfers between devices, swap(): return lax.ppermute(values, axis, [(i, i ^ 1) for i in range(count)])  119 us
    dot_general x12, matrix products, dot(): lax.dot_general(a, b, (((da,), (db,)), ((), ())), preferred_element_type=...  64.3 us
    all_gather x2, waiting for transfers between devices, gather_rows(): part = lax.all_gather(shard, SAME, axis=0, tiled=False)  57.6 us
    all_to_all x3, waiting for transfers between devices, trade(): return lax.all_to_all(values, CTX, split_axis=0, concat_axis=0, tiled=True)  51.3 us
    all_to_all x1, blocking collectives, trade(): return lax.all_to_all(values, CTX, split_axis=0, concat_axis=0, tiled=True)  48.7 us
    pallas_call x1, Pallas kernels, attend_backward(): pl.pallas_call(backward_kernel, grid=(seqs,), in_specs=[wide, pl.BlockSpe...  22.7 us
    ppermute x8, waiting for transfers between devices, small_sums(): total = total + lax.ppermute(total, axis, pairs)  21.7 us
    concatenate x1, other arithmetic, local(): early = jnp.concatenate([grad_down, grad_up, grad_out], 1)  19.8 us
  transfers between devices with their start and end apart: 23, of which 18 were waited for; matrix products, arithmetic and copies ran while one was open for 19% of the time, Pallas kernels for 7%

profile of v2, /device:TPU:0, one launch (start us, length us, event | category | flops | bytes accessed | tf_op | source)
XLA Modules:
  0.0 564.0 jit_solution(3970545912665366338)
XLA Ops:
  12.2 50.5 %all-gather.5.cloned.1.call-done = bf16[512,2048]{1,0:T(8,128)(2,1)} async-done(((bf16[64,2048]{1,0:T(8,128)(2,1)}), bf16[512,2048]{1,0:T(8,128)(2,1)}) %all-gather.5.cloned.1.call-update) | async-done | bytes 2097168 | tf_op jit(solution)/shard_map/all_gather | solution.py:203
  64.7 2.6 collective-permute-done
  69.8 3.2 add_convert_fusion
  74.8 3.8 all-to-all-start
  80.7 40.3 %all-to-all-done = bf16[4,864,384]{2,1,0:T(8,128)(2,1)S(1)} async-done(((bf16[4,864,384]{2,1,0:T(8,128)(2,1)}), bf16[4,864,384]{2,1,0:T(8,128)(2,1)S(1)}, u32[]{:S(2)}, u32[]{:S(2)}) %all-to-all-start) | async-done | bytes 2654240 | tf_op jit(solution)/shard_map/all_to_all | solution.py:186
  121.0 15.1 %shard_map.254 = (bf16[4,3,288,128]{3,2,1,0:T(8,128)(2,1)}, f32[3,2,1152]{2,1,0:T(2,128)S(1)}) custom-call(bf16[4,3,288,384]{3,2,1,0:T(8,128)(2,1)S(1)} %bitcast.121, s32[3,1,1152]{2,1,0:T(1,128)S(1)} %broadcast_in_dim.2.start_ref), custom_call_target="tpu_custom_call" | custom-call | flops 8153726976 | bytes 3538944 | tf_op jit(solution)/shard_map/pallas_call | solution.py:128
  136.1 4.4 all-to-all-start.1
  140.6 7.1 %all-gather.7.cloned.1.call-done = bf16[512,4096]{1,0:T(8,128)(2,1)} async-done(((bf16[64,4096]{1,0:T(8,128)(2,1)}), bf16[512,4096]{1,0:T(8,128)(2,1)}) %all-gather.7.cloned.1.call-update) | async-done | bytes 4194320 | tf_op jit(solution)/shard_map/all_gather | solution.py:203
  147.6 5.7 %all-to-all-done.1 = bf16[4,864,128]{2,1,0:T(8,128)(2,1)} async-done(((bf16[4,864,128]{2,1,0:T(8,128)(2,1)}), bf16[4,864,128]{2,1,0:T(8,128)(2,1)}, u32[]{:S(2)}, u32[]{:S(2)}) %all-to-all-start.1) | async-done | bytes 884768 | tf_op jit(solution)/shard_map/all_to_all | solution.py:186
  153.3 2.5 copy.78
  155.8 2.4 dot_general.43
  158.3 3.8 convolution_convert_fusion.2
  165.8 36.8 %collective-permute-done.1 = bf16[3,288,1024]{2,1,0:T(8,128)(2,1)} collective-permute-done((bf16[3,288,1024]{2,1,0:T(8,128)(2,1)}, bf16[3,288,1024]{2,1,0:T(8,128)(2,1)}, u32[]{:S(2)}, u32[]{:S(2)}) %collective-permute-start.1) | collective-permute-done | bytes 1769504 | tf_op jit(solution)/shard_map/ppermute | solution.py:182
  202.6 3.4 fusion.62
  209.5 5.1 select_bitcast_fusion.1
  214.6 7.6 %pad_maximum_fusion.1 = bf16[8,2,64,4096]{3,2,1,0:T(8,128)(2,1)} fusion(bf16[8,1,64,4096]{3,2,1,0:T(8,128)(2,1)} %get-tuple-element.43, bf16[8,1,64,4096]{3,2,1,0:T(8,128)(2,1)} %get-tuple-element.42), kind=kLoop, calls=%fused_computation.6 | loop fusion | flops 4194304 | bytes 16777216 | tf_op jit(solution)/shard_map/stack | solution.py:208
  222.2 5.8 %fusion.18 = f32[864,2048]{1,0:T(8,128)S(1)} fusion(bf16[864,1024]{1,0:T(8,128)(2,1)S(1)} %bitcast.153, bf16[1024,4096]{1,0:T(8,128)(2,1)} %bitcast.131), kind=kOutput, calls=%fused_computation.41 | convolution fusion | flops 3623878656 | bytes 13041664 | tf_op jit(solution)/shard_map/dot_general | solution.py:45
  228.1 9.2 %fusion.67 = (f32[2048]{0:T(1024)}, bf16[864,2048]{1,0:T(8,128)(2,1)S(1)}) fusion(f32[864,2048]{1,0:T(8,128)S(1)} %fusion.18, f32[2048]{0:T(1024)S(1)} %copy-done.40, bf16[864,1024]{1,0:T(8,128)(2,1)S(1)} %bitcast.159, bf16[1024,4096]{1,0:T(8,128)(2,1)S(1)} %bitcast.133), kind=kOutput, calls=%fused_computation.119 | convolution fusion | flops 3662804992 | bytes 16596992 | tf_op jit(solution)/shard_map/dot_general | solution.py:45
  237.3 3.9 fusion.51
  242.7 5.3 convolution_convert_fusion.1
  248.0 9.1 %convert_bitcast_fusion = bf16[1024,2048]{0,1:T(8,128)(2,1)S(1)} fusion(bf16[864,1024]{1,0:T(8,128)(2,1)S(1)} %bitcast.160, f32[864,2048]{1,0:T(8,128)} %copy-done.41, f32[2048]{0:T(1024)S(1)} %copy-done.40), kind=kOutput, calls=%fused_computation.34 | convolution fusion | flops 3643670528 | bytes 13049856 | tf_op jit(solution)/shard_map/dot_general | solution.py:45
  257.1 23.3 %collective-permute-done.3 = bf16[3,288,1024]{2,1,0:T(8,128)(2,1)S(1)} collective-permute-done((bf16[3,288,1024]{2,1,0:T(8,128)(2,1)S(1)}, bf16[3,288,1024]{2,1,0:T(8,128)(2,1)S(1)}, u32[]{:S(2)}, u32[]{:S(2)}) %collective-permute-start.3) | collective-permute-done | bytes 1769504 | tf_op jit(solution)/shard_map/ppermute | solution.py:182
  280.4 2.6 multiply_reduce_fusion
  283.1 2.5 fusion.61
  289.0 19.8 %pad_maximum_fusion = bf16[1024,4608]{0,1:T(8,128)(2,1)} fusion(bf16[1024,512]{0,1:T(8,128)(2,1)S(1)} %convolution_convert_fusion.3, bf16[1024,2048]{0,1:T(8,128)(2,1)S(1)} %convolution_convert_fusion.1, bf16[1024,2048]{0,1:T(8,128)(2,1)S(1)} %convert_bitcast_fusion), kind=kLoop, calls=%fused_computation.3 | loop fusion | flops 28311552 | bytes 18874368 | tf_op jit(solution)/shard_map/concatenate | solution.py:316
  308.7 12.5 %copy.83 = bf16[1024,4608]{1,0:T(8,128)(2,1)} copy(bf16[1024,4608]{0,1:T(8,128)(2,1)} %pad_maximum_fusion) | data formatting | bytes 18874368 | tf_op jit(solution)/shard_map/concatenate | solution.py:316
  321.2 4.9 dynamic-slice_bitcast_fusion
  326.1 10.1 %fusion.48 = bf16[864,1024]{1,0:T(8,128)(2,1)} fusion(bf16[1024,4096]{1,0:T(8,128)(2,1)} %bitcast.132, f32[864,2048]{1,0:T(8,128)} %copy-done.41, f32[2048]{0:T(1024)S(1)} %copy-done.40), kind=kOutput, calls=%fused_computation.82 | convolution fusion | flops 3642458112 | bytes 13049856 | tf_op jit(solution)/shard_map/dot_general | solution.py:45
  339.6 3.5 all-to-all-start.2
  343.2 7.3 %fusion = bf16[8,64,4608]{2,1,0:T(8,128)(2,1)} fusion(bf16[8,64,4608]{2,1,0:T(8,128)(2,1)} %collective-permute-done.4, bf16[8,2,64,4608]{3,2,1,0:T(8,128)(2,1)} %bitcast.128, s32[]{:T(128)S(6)} %select_n.40), kind=kLoop, calls=%fused_computation.5 | loop fusion | flops 9437184 | bytes 14155780 | tf_op jit(solution)/shard_map/convert_element_type | solution.py:218
  350.5 5.3 all-to-all-done.2
  356.7 22.7 %shard_map.255 = bf16[4,3,288,384]{3,2,1,0:T(8,128)(2,1)S(1)} custom-call(bf16[4,3,288,384]{3,2,1,0:T(8,128)(2,1)S(1)} %bitcast.122, s32[3,1,1152]{2,1,0:T(1,128)S(1)} %broadcast_in_dim.2.start_ref, f32[3,2,1152]{2,1,0:T(2,128)S(1)} %copy-done.1, bf16[4,3,288,128]{3,2,1,0:T(8,128)(2,1)S(1)} %bitcast.124), custom_call_target="tpu_custom_call" | custom-call | flops 20384317440 | bytes 6193152 | tf_op jit(solution)/shard_map/pallas_call | solution.py:157
  379.3 48.7 %all_to_all.20 = bf16[4,864,384]{2,1,0:T(8,128)(2,1)S(1)} all-to-all(bf16[4,864,384]{2,1,0:T(8,128)(2,1)S(1)} %bitcast.123), channel_id=1, replica_groups=mesh['fsdp'=4,'x'=2,'core'=2,'tp'=2] {'x','core'}, dimensions={0} | all-to-all | bytes 5308416 | tf_op jit(solution)/shard_map/all_to_all | solution.py:186
  428.0 2.8 copy.84
  430.9 2.8 copy.85
  433.6 5.6 %dot_general.54 = bf16[3,288,1536]{2,1,0:T(8,128)(2,1)} reshape(bf16[864,4,384]{2,1,0:T(4,128)(2,1)} %copy.84) | data formatting | bytes 5308416 | tf_op jit(solution)/shard_map/dot_general | solution.py:45
  439.3 5.9 %convolution_convert_fusion = bf16[1024,1536]{1,0:T(8,128)(2,1)S(1)} fusion(bf16[864,1024]{1,0:T(8,128)(2,1)} %bitcast.156, bf16[864,1536]{0,1:T(8,128)(2,1)} %bitcast.148), kind=kOutput, calls=%fused_computation.37 | convolution fusion | flops 2719481856 | bytes 7569408 | tf_op jit(solution)/shard_map/dot_general | solution.py:45
  445.6 4.4 fusion.45
  452.6 5.5 collective-permute-done.12
  458.2 4.7 collective-permute-done.13
  462.9 3.8 collective-permute-done.14
  472.9 19.0 %collective-permute-done.6 = bf16[3,288,1024]{2,1,0:T(8,128)(2,1)} collective-permute-done((bf16[3,288,1024]{2,1,0:T(8,128)(2,1)}, bf16[3,288,1024]{2,1,0:T(8,128)(2,1)}, u32[]{:S(2)}, u32[]{:S(2)}) %collective-permute-start.6) | collective-permute-done | bytes 1769504 | tf_op jit(solution)/shard_map/ppermute | solution.py:182
  492.0 37.3 %collective-permute-done.5 = bf16[3,288,1024]{2,1,0:T(8,128)(2,1)} collective-permute-done((bf16[3,288,1024]{2,1,0:T(8,128)(2,1)}, bf16[3,288,1024]{2,1,0:T(8,128)(2,1)}, u32[]{:S(2)}, u32[]{:S(2)}) %collective-permute-start.5) | collective-permute-done | bytes 1769504 | tf_op jit(solution)/shard_map/ppermute | solution.py:182
  529.2 4.2 add_convert_fusion.1
  534.9 4.2 fusion.29
  539.7 3.3 collective-permute-done.8
  544.2 4.2 fusion.28
  549.5 2.6 collective-permute-done.10
  (177 shorter events, 47.8 us)
Async XLA Ops:
  7.2 55.7 %copy-start.38 = (f32[2,512]{1,0:T(2,128)S(1)}, f32[2,512]{1,0:T(2,128)}, u32[]{:S(2)}) copy-start(f32[2,512]{1,0:T(2,128)} %param.20) | copy-start | bytes 12292
  7.2 55.7 %copy-start.5 = (bf16[3,288,1024]{2,1,0:T(8,128)(2,1)S(1)}, bf16[3,288,1024]{2,1,0:T(8,128)(2,1)}, u32[]{:S(2)}) copy-start(bf16[3,288,1024]{2,1,0:T(8,128)(2,1)} %param.15) | copy-start | bytes 5308420
  7.2 55.6 %all-gather.5.cloned.1.call-start = ((), (), s32[]{:S(2)}) async-start(), calls=%async_computation.8 | async-start | bytes 2359296 | tf_op jit(solution)/shard_map/all_gather | solution.py:203
  8.3 55.6 %copy-start.28 = (f32[1024]{0:T(1024)S(1)}, f32[1024]{0:T(1024)}, u32[]{:S(2)}) copy-start(f32[1024]{0:T(1024)} %param.17) | copy-start | bytes 12292
  8.4 55.6 %copy-start.39 = (f32[1024]{0:T(1024)S(1)}, f32[1024]{0:T(1024)}, u32[]{:S(2)}) copy-start(f32[1024]{0:T(1024)} %param.18) | copy-start | bytes 12292
  10.3 137.3 %all-gather.7.cloned.1.call-start = ((), (), s32[]{:S(2)}) async-start(), calls=%async_computation.9 | async-start | bytes 4718592 | tf_op jit(solution)/shard_map/all_gather | solution.py:203
  62.8 4.5 collective-permute-start
  63.3 6.1 %copy-start.23 = (f32[3,288]{1,0:T(4,128)}, f32[3,288]{1,0:T(4,128)S(1)}, u32[]{:S(2)}) copy-start(f32[3,288]{1,0:T(4,128)S(1)} %broadcast_multiply_fusion.5) | copy-start | bytes 10372
  74.8 46.3 %all-to-all-start = ((bf16[4,864,384]{2,1,0:T(8,128)(2,1)}), bf16[4,864,384]{2,1,0:T(8,128)(2,1)S(1)}, u32[]{:S(2)}, u32[]{:S(2)}) async-start(bf16[4,864,384]{2,1,0:T(8,128)(2,1)} %bitcast.130), calls=%async_computation | async-start | bytes 5308416 | tf_op jit(solution)/shard_map/all_to_all | solution.py:186
  136.1 26.0 %copy-start = (f32[3,2,1152]{2,1,0:T(2,128)}, f32[3,2,1152]{2,1,0:T(2,128)S(1)}, u32[]{:S(2)}) copy-start(f32[3,2,1152]{2,1,0:T(2,128)S(1)} %get-tuple-element.24.lse_ref) | copy-start | bytes 82948
  136.1 17.2 %all-to-all-start.1 = ((bf16[4,864,128]{2,1,0:T(8,128)(2,1)}), bf16[4,864,128]{2,1,0:T(8,128)(2,1)}, u32[]{:S(2)}, u32[]{:S(2)}) async-start(bf16[4,864,128]{2,1,0:T(8,128)(2,1)} %bitcast.12), calls=%async_computation.1 | async-start | bytes 1769472 | tf_op jit(solution)/shard_map/all_to_all | solution.py:186
  147.6 60.2 %collective-permute-start.2 = (bf16[8,64,4096]{2,1,0:T(8,128)(2,1)}, bf16[8,64,4096]{2,1,0:T(8,128)(2,1)}, u32[]{:S(2)}, u32[]{:S(2)}) collective-permute-start(bf16[8,64,4096]{2,1,0:T(8,128)(2,1)} %bitcast.139), channel_id=1, source_target_pairs={{0,2},{2,0},{1,3},{3,1},{4,6},{6,4},{5,7},{7,5},{8,10},{10,8},{9,1... | collective-permute-start | bytes 12582920 | tf_op jit(solution)/shard_map/ppermute | solution.py:182
  158.3 44.3 %copy-start.36 = (f32[1024]{0:T(1024)S(1)}, f32[1024]{0:T(1024)}, u32[]{:S(2)}) copy-start(f32[1024]{0:T(1024)} %param.22) | copy-start | bytes 12292
  162.1 40.5 %collective-permute-start.1 = (bf16[3,288,1024]{2,1,0:T(8,128)(2,1)}, bf16[3,288,1024]{2,1,0:T(8,128)(2,1)}, u32[]{:S(2)}, u32[]{:S(2)}) collective-permute-start(bf16[3,288,1024]{2,1,0:T(8,128)(2,1)} %convolution_convert_fusion.2), channel_id=1, source_target_pairs={{0,1},{1,0},{2,3},{3,2},{4,5},{5,4},{6,7},{7,6},{8,9},{9,8},{10,11... | collective-permute-start | bytes 5308424 | tf_op jit(solution)/shard_map/ppermute | solution.py:182
  222.2 5.8 %copy-start.21 = (bf16[3,288,1024]{2,1,0:T(8,128)(2,1)S(1)}, bf16[3,288,1024]{2,1,0:T(8,128)(2,1)}, u32[]{:S(2)}) copy-start(bf16[3,288,1024]{2,1,0:T(8,128)(2,1)} %param.29) | copy-start | bytes 5308420
  222.2 5.8 %copy-start.40 = (f32[2048]{0:T(1024)S(1)}, f32[2048]{0:T(1024)}, u32[]{:S(2)}) copy-start(f32[2048]{0:T(1024)} %param.26) | copy-start | bytes 24580
  228.0 9.2 %copy-start.41 = (f32[864,2048]{1,0:T(8,128)}, f32[864,2048]{1,0:T(8,128)S(1)}, u32[]{:S(2)}) copy-start(f32[864,2048]{1,0:T(8,128)S(1)} %fusion.18) | copy-start | bytes 21233668
  241.1 39.3 %collective-permute-start.3 = (bf16[3,288,1024]{2,1,0:T(8,128)(2,1)S(1)}, bf16[3,288,1024]{2,1,0:T(8,128)(2,1)S(1)}, u32[]{:S(2)}, u32[]{:S(2)}) collective-permute-start(bf16[3,288,1024]{2,1,0:T(8,128)(2,1)S(1)} %bitcast.135), channel_id=1, source_target_pairs={{0,1},{1,0},{2,3},{3,2},{4,5},{5,4},{6,7},{7,6},{8,9},{9,8},{10,11... | collective-permute-start | bytes 5308424 | tf_op jit(solution)/shard_map/ppermute | solution.py:182
  248.0 32.5 %copy-start.3 = (f32[3,288,1024]{2,1,0:T(8,128)S(1)}, f32[3,288,1024]{2,1,0:T(8,128)}, u32[]{:S(2)}) copy-start(f32[3,288,1024]{2,1,0:T(8,128)} %copy-done.2) | copy-start | bytes 10616836
  326.1 17.1 %collective-permute-start.4 = (bf16[8,64,4608]{2,1,0:T(8,128)(2,1)}, bf16[8,64,4608]{2,1,0:T(8,128)(2,1)}, u32[]{:S(2)}, u32[]{:S(2)}) collective-permute-start(bf16[8,64,4608]{2,1,0:T(8,128)(2,1)} %dynamic-slice_bitcast_fusion), channel_id=1, source_target_pairs={{0,2},{2,0},{1,3},{3,1},{4,6},{6,4},{5,7},{7,5},{8,10},{10,8},{9,1... | collective-permute-start | bytes 14155784 | tf_op jit(solution)/shard_map/ppermute | solution.py:182
  326.1 10.1 %copy-start.20 = (bf16[3,288,1024]{2,1,0:T(8,128)(2,1)S(1)}, bf16[3,288,1024]{2,1,0:T(8,128)(2,1)}, u32[]{:S(2)}) copy-start(bf16[3,288,1024]{2,1,0:T(8,128)(2,1)} %copy-done.19) | copy-start | bytes 5308420
  339.6 16.2 %all-to-all-start.2 = ((bf16[4,864,128]{2,1,0:T(8,128)(2,1)}), bf16[4,864,128]{2,1,0:T(8,128)(2,1)S(1)}, u32[]{:S(2)}, u32[]{:S(2)}) async-start(bf16[4,864,128]{2,1,0:T(8,128)(2,1)} %bitcast.145), calls=%async_computation.2 | async-start | bytes 1769472 | tf_op jit(solution)/shard_map/all_to_all | solution.py:186
  343.2 127.6 %reduce-scatter.3.cloned.1.call-start = ((), (), s32[]{:S(2)}) async-start(), calls=%async_computation.6 | async-start | bytes 5308416 | tf_op jit(solution)/shard_map/reduce_scatter | solution.py:223
  355.9 198.9 %reduce-scatter.5.cloned.1.call-start = ((), (), s32[]{:S(2)}) async-start(), calls=%async_computation.7 | async-start | bytes 1769472 | tf_op jit(solution)/shard_map/reduce_scatter | solution.py:223
  439.3 6.4 %copy-start.15 = (bf16[8,2,64,2048]{3,2,1,0:T(8,128)(2,1)S(1)}, bf16[8,2,64,2048]{3,2,1,0:T(8,128)(2,1)}, u32[]{:S(2)}) copy-start(bf16[8,2,64,2048]{3,2,1,0:T(8,128)(2,1)} %copy-done.14) | copy-start | bytes 12582916
  439.3 6.4 %copy-start.16 = (bf16[3,288,1536]{2,1,0:T(8,128)(2,1)S(1)}, bf16[3,288,1536]{2,1,0:T(8,128)(2,1)}, u32[]{:S(2)}) copy-start(bf16[3,288,1536]{2,1,0:T(8,128)(2,1)} %dot_general.54) | copy-start | bytes 7962628
  445.4 6.8 %copy-start.35 = (f32[2048]{0:T(1024)S(1)}, f32[2048]{0:T(1024)}, u32[]{:S(2)}) copy-start(f32[2048]{0:T(1024)} %get-tuple-element.58) | copy-start | bytes 24580
  445.4 6.8 %copy-start.34 = (f32[1024]{0:T(1024)S(1)}, f32[1024]{0:T(1024)}, u32[]{:S(2)}) copy-start(f32[1024]{0:T(1024)} %get-tuple-element.46) | copy-start | bytes 12292
  445.4 6.8 %copy-start.33 = (f32[1024]{0:T(1024)S(1)}, f32[1024]{0:T(1024)}, u32[]{:S(2)}) copy-start(f32[1024]{0:T(1024)} %get-tuple-element.38) | copy-start | bytes 12292
  445.4 6.8 %copy-start.32 = (f32[1024]{0:T(1024)S(1)}, f32[1024]{0:T(1024)}, u32[]{:S(2)}) copy-start(f32[1024]{0:T(1024)} %get-tuple-element.30) | copy-start | bytes 12292
  445.4 6.8 %copy-start.31 = (f32[1024]{0:T(1024)S(1)}, f32[1024]{0:T(1024)}, u32[]{:S(2)}) copy-start(f32[1024]{0:T(1024)} %get-tuple-element.36) | copy-start | bytes 12292
  445.4 23.7 %collective-permute-start.7 = (bf16[8,64,1536]{2,1,0:T(8,128)(2,1)S(1)}, bf16[8,64,1536]{2,1,0:T(8,128)(2,1)S(1)}, u32[]{:S(2)}, u32[]{:S(2)}) collective-permute-start(bf16[8,64,1536]{2,1,0:T(8,128)(2,1)S(1)} %dynamic-slice_bitcast_fusion.1), channel_id=1, source_target_pairs={{0,2},{2,0},{1,3},{3,1},{4,6},{6,4},{5,7},{7,5},{8,10},{10,8},{9,1... | collective-permute-start | bytes 4718600 | tf_op jit(solution)/shard_map/ppermute | solution.py:182
  450.1 41.8 %collective-permute-start.6 = (bf16[3,288,1024]{2,1,0:T(8,128)(2,1)}, bf16[3,288,1024]{2,1,0:T(8,128)(2,1)}, u32[]{:S(2)}, u32[]{:S(2)}) collective-permute-start(bf16[3,288,1024]{2,1,0:T(8,128)(2,1)} %fusion.45), channel_id=1, source_target_pairs={{0,1},{1,0},{2,3},{3,2},{4,5},{5,4},{6,7},{7,6},{8,9},{9,8},{10,11... | collective-permute-start | bytes 5308424 | tf_op jit(solution)/shard_map/ppermute | solution.py:182
  451.6 77.7 %collective-permute-start.5 = (bf16[3,288,1024]{2,1,0:T(8,128)(2,1)}, bf16[3,288,1024]{2,1,0:T(8,128)(2,1)}, u32[]{:S(2)}, u32[]{:S(2)}) collective-permute-start(bf16[3,288,1024]{2,1,0:T(8,128)(2,1)} %bitcast.34), channel_id=1, source_target_pairs={{0,1},{1,0},{2,3},{3,2},{4,5},{5,4},{6,7},{7,6},{8,9},{9,8},{10,11... | collective-permute-start | bytes 5308424 | tf_op jit(solution)/shard_map/ppermute | solution.py:182
  452.3 5.9 %collective-permute-start.12 = (f32[6144]{0:T(1024)S(1)}, f32[6144]{0:T(1024)S(1)}, u32[]{:S(2)}, u32[]{:S(2)}) collective-permute-start(f32[6144]{0:T(1024)S(1)} %constant_dynamic-update-slice_fusion), channel_id=1, source_target_pairs={{0,8},{8,0},{16,24},{24,16},{1,9},{9,1},{17,25},{25,17},{2,10},{10... | collective-permute-start | bytes 73736 | tf_op jit(solution)/shard_map/ppermute | solution.py:234
  458.2 4.7 collective-permute-start.13
  462.9 3.8 collective-permute-start.14
  466.7 1.2 collective-permute-start.15
  469.1 60.1 %copy-start.4 = (f32[3,288,1024]{2,1,0:T(8,128)S(1)}, f32[3,288,1024]{2,1,0:T(8,128)}, u32[]{:S(2)}) copy-start(f32[3,288,1024]{2,1,0:T(8,128)} %copy-done.2) | copy-start | bytes 10616836
  491.9 41.5 %copy-start.8 = (bf16[4,864,384]{2,1,0:T(8,128)(2,1)S(1)}, bf16[4,864,384]{2,1,0:T(8,128)(2,1)}, u32[]{:S(2)}) copy-start(bf16[4,864,384]{2,1,0:T(8,128)(2,1)} %copy-done.7) | copy-start | bytes 7962628
  491.9 41.9 %copy-start.24 = (f32[3,288]{1,0:T(4,128)S(1)}, f32[3,288]{1,0:T(4,128)}, u32[]{:S(2)}) copy-start(f32[3,288]{1,0:T(4,128)} %copy-done.23) | copy-start | bytes 10372
  491.9 41.9 %copy-start.26 = (f32[3,288]{1,0:T(4,128)S(1)}, f32[3,288]{1,0:T(4,128)}, u32[]{:S(2)}) copy-start(f32[3,288]{1,0:T(4,128)} %copy-done.25) | copy-start | bytes 10372
  533.5 10.7 %copy-start.29 = (f32[1024]{0:T(1024)S(1)}, f32[1024]{0:T(1024)}, u32[]{:S(2)}) copy-start(f32[1024]{0:T(1024)} %param.17) | copy-start | bytes 12292
  533.9 10.3 %copy-start.10 = (f32[3,288,1024]{2,1,0:T(8,128)S(1)}, f32[3,288,1024]{2,1,0:T(8,128)}, u32[]{:S(2)}) copy-start(f32[3,288,1024]{2,1,0:T(8,128)} %copy-done.9) | copy-start | bytes 10616836
  539.2 3.8 collective-permute-start.8
  542.9 5.4 collective-permute-start.9
  548.4 3.8 collective-permute-start.10
  552.1 1.2 collective-permute-start.11
  (17 other events, 52.4 us)
Sparse Core Ops, SparseCore 0:
  10.7 51.9 all-gather.4
  65.5 82.1 all-gather.6
  356.0 104.2 reduce-scatter.2
  492.0 62.6 reduce-scatter.4
